TPU v7x, 512 devices: a whole 4x8x8 slice. The times are simulated.
512 devices in a mesh: dp: 8 (over z_hi, core), seq: 64 (over z_lo, y, x).
Axes of the slice: x: 4, y: 8, z: 8 (z_hi: 4, z_lo: 2; z = z_hi * 2 + z_lo), core: 2. Of those that a mesh axis runs over, the one named last changes fastest.
Arguments:
- query_gate: bfloat16 [8, 16384, 256], P('dp', 'seq'), may hold values from -6 to 6
- key_gate: bfloat16 [8, 16384, 256], P('dp', 'seq'), may hold values from -6 to 6
- values_in: bfloat16 [8, 16384, 256], P('dp', 'seq'), may hold values from -6 to 6
- grad_out: bfloat16 [8, 16384, 256], P('dp', 'seq'), may hold values from -6 to 6
- long_filter: bfloat16 [16384, 256], P('seq'), may hold values from -6 to 6
Outputs:
- grad_query: bfloat16 [8, 16384, 256], P('dp', 'seq')
- grad_key: bfloat16 [8, 16384, 256], P('dp', 'seq')
- grad_value: bfloat16 [8, 16384, 256], P('dp', 'seq')
- grad_filter: float32 [16384, 256], P('seq')
All inputs are finite; a program needn't handle non-finite values.
Results may differ from a plain program's by a relative error of at most 0.0049.
Values may be sent and summed in bfloat16 or wider, within the bound.
No kernel may reach another device: no remote copies, remote signals or barrier semaphores. Data moves between devices by JAX's collectives and lax.ppermute only.
A program may use at most 64 MiB of HBM per device.

v0:
```python
import math

import jax
import jax.numpy as jnp
from jax import lax
from jax.sharding import PartitionSpec as P

highest_precision = lax.Precision.HIGHEST


def phase_table(first_positions, second_positions, period, angle_sign):
    product = first_positions[:, None] * second_positions[None, :] % period
    angles = angle_sign * 2.0 * math.pi / period * product.astype(jnp.float32)
    return (jnp.cos(angles), jnp.sin(angles))


def twist(paired, cosine, sine_part):
    return jnp.stack(
        [paired[0] * cosine - paired[1] * sine_part, paired[0] * sine_part + paired[1] * cosine]
    )


def block_matrix(count, angle_sign):
    positions = jnp.arange(count, dtype=jnp.int32)
    cosine, sine_part = phase_table(positions, positions, count, angle_sign)
    return jnp.stack([jnp.stack([cosine, sine_part]), jnp.stack([-sine_part, cosine])])


def first_half(signal, row_start, period):
    blocks = signal.shape[0]
    freq_positions = jnp.arange(2 * blocks, dtype=jnp.int32)
    cosine, sine_part = phase_table(
        jnp.arange(blocks, dtype=jnp.int32), freq_positions, 2 * blocks, -1.0
    )
    paired = jnp.einsum(
        "nrc,snf->sfrc", signal, jnp.stack([cosine, sine_part]), precision=highest_precision
    )
    row_positions = row_start + jnp.arange(signal.shape[1], dtype=jnp.int32)
    tw_cos, tw_sin = phase_table(freq_positions, row_positions, period, -1.0)
    return twist(paired, tw_cos[:, :, None], tw_sin[:, :, None])


def row_transform(paired, angle_sign):
    matrix = block_matrix(paired.shape[2], angle_sign)
    return jnp.einsum("sfrc,strg->tfgc", paired, matrix, precision=highest_precision)


def invert_rows(paired, freq_start, period):
    paired = row_transform(paired, 1.0)
    freq_positions = freq_start + jnp.arange(paired.shape[1], dtype=jnp.int32)
    row_positions = jnp.arange(paired.shape[2], dtype=jnp.int32)
    tw_cos, tw_sin = phase_table(freq_positions, row_positions, period, 1.0)
    return twist(paired, tw_cos[:, :, None], tw_sin[:, :, None])


def invert_blocks(paired, period):
    freq_count = paired.shape[1]
    cosine, sine_part = phase_table(
        jnp.arange(freq_count, dtype=jnp.int32),
        jnp.arange(freq_count // 2, dtype=jnp.int32),
        freq_count,
        1.0,
    )
    result = jnp.einsum(
        "sfrc,sfn->nrc", paired, jnp.stack([cosine, -sine_part]), precision=highest_precision
    )
    return result / period


def multiply(left_spec, right_spec):
    return jnp.stack(
        [
            left_spec[0] * right_spec[0] - left_spec[1] * right_spec[1],
            left_spec[0] * right_spec[1] + left_spec[1] * right_spec[0],
        ]
    )


def multiply_conj(left_spec, right_spec):
    return jnp.stack(
        [
            left_spec[0] * right_spec[0] + left_spec[1] * right_spec[1],
            left_spec[1] * right_spec[0] - left_spec[0] * right_spec[1],
        ]
    )


def spectral_products(spectra, axis_index):
    spec_mixed, spec_gated, spec_filter = jnp.split(spectra, 3, axis=axis_index)
    parts_list = [
        multiply(spec_mixed, spec_filter),
        multiply_conj(spec_gated, spec_filter),
        multiply_conj(spec_gated, spec_mixed),
    ]
    return jnp.concatenate(parts_list, axis=axis_index)


def body(query_gate, key_gate, values_in, grad_out, long_filter):
    shards = lax.axis_size("seq")
    position = lax.axis_index("seq")
    num_rows = query_gate.shape[1]
    channels = query_gate.shape[2]
    length_fft = 2 * num_rows * shards
    scaling = 1.0 / math.sqrt(num_rows * shards)
    mixed_in = (key_gate.astype(jnp.float32) * values_in.astype(jnp.float32)).astype(jnp.bfloat16)
    gated_grad = (grad_out.astype(jnp.float32) * query_gate.astype(jnp.float32)).astype(
        jnp.bfloat16
    )
    combined = jnp.concatenate([mixed_in, gated_grad, long_filter[None]], axis=2)
    rows_in = lax.all_to_all(combined, "seq", split_axis=1, concat_axis=0, tiled=True)
    channel_scale = jnp.concatenate(
        [jnp.ones((2 * channels,), jnp.float32), jnp.full((channels,), scaling, jnp.float32)]
    )
    row_start = position * (num_rows // shards)
    half = first_half(rows_in.astype(jnp.float32) * channel_scale, row_start, length_fft)
    moved = lax.all_to_all(half, "seq", split_axis=1, concat_axis=2, tiled=True)
    spectra = row_transform(moved, -1.0)
    products = spectral_products(spectra, 3)
    freq_start = position * moved.shape[1]
    back = invert_rows(products, freq_start, length_fft)
    returned = lax.all_to_all(back, "seq", split_axis=2, concat_axis=1, tiled=True)
    blocks = invert_blocks(returned, length_fft)
    signals = lax.all_to_all(blocks, "seq", split_axis=0, concat_axis=1, tiled=True)
    conv_out = signals[:, :, :channels]
    grad_mixed = signals[:, :, channels : 2 * channels]
    filter_part = signals[:, :, 2 * channels :]
    grad_filter = lax.psum(filter_part[0] * scaling, "dp")
    grad_query = (grad_out.astype(jnp.float32) * conv_out).astype(jnp.bfloat16)
    grad_key = (grad_mixed * values_in.astype(jnp.float32)).astype(jnp.bfloat16)
    grad_value = (grad_mixed * key_gate.astype(jnp.float32)).astype(jnp.bfloat16)
    return (grad_query, grad_key, grad_value, grad_filter)


def solution(mesh):
    return jax.shard_map(
        body,
        mesh=mesh,
        in_specs=(
            P("dp", "seq", None),
            P("dp", "seq", None),
            P("dp", "seq", None),
            P("dp", "seq", None),
            P("seq", None),
        ),
        out_specs=(
            P("dp", "seq", None),
            P("dp", "seq", None),
            P("dp", "seq", None),
            P("seq", None),
        ),
        check_vma=False,
    )
```

profile of v0, /device:TPU:1, one launch (start us, length us, event | category | flops | bytes accessed | tf_op | source)
XLA Modules:
  0.0 359.5 jit_solution(17217223660758418960)
XLA Ops:
  7.2 1.2 fusion.13
  8.3 0.9 pad_maximum_fusion.2
  10.4 3.0 reduce.2
  13.4 1.0 reshape.393
  14.4 13.2 %all-to-all-start = ((bf16[64,2,1536]{2,1,0:T(2,128)(2,1)}), bf16[64,2,1536]{2,1,0:T(2,128)(2,1)S(1)}, u32[]{:S(2)}, u32[]{:S(2)}) async-start(bf16[64,2,1536]{2,1,0:T(2,128)(2,1)} %reshape.393), calls=%async_computation | async-start | bytes 786432 | tf_op jit(solution)/shard_map/all_to_all | solution.py:110
  27.9 12.5 %all-to-all-done = bf16[64,2,1536]{2,1,0:T(2,128)(2,1)S(1)} async-done(((bf16[64,2,1536]{2,1,0:T(2,128)(2,1)}), bf16[64,2,1536]{2,1,0:T(2,128)(2,1)S(1)}, u32[]{:S(2)}, u32[]{:S(2)}) %all-to-all-start) | async-done | bytes 393248 | tf_op jit(solution)/shard_map/all_to_all | solution.py:110
  40.8 2.2 convert_reduce_fusion
  43.2 2.7 fusion.10
  46.6 3.7 %copy.25 = f32[2,128,4,768]{3,2,0,1:T(4,128)} copy(f32[2,128,4,768]{3,1,2,0:T(8,128)S(1)} %pad_maximum_fusion) | data formatting | bytes 6291456 | tf_op jit(solution)/shard_map/stack | solution.py:18
  50.3 7.8 %all-to-all-start.1 = ((f32[2,128,4,768]{3,2,0,1:T(4,128)}), f32[2,128,4,768]{3,2,0,1:T(4,128)S(1)}, u32[]{:S(2)}, u32[]{:S(2)}) async-start(f32[2,128,4,768]{3,2,0,1:T(4,128)} %copy.25), calls=%async_computation.1 | async-start | bytes 6291456 | tf_op jit(solution)/shard_map/all_to_all | solution.py:116
  58.1 1.0 fusion.25
  59.0 1.0 fusion.24
  60.0 1.0 multiply_sine_fusion
  61.1 1.0 multiply_sine_fusion.1
  62.1 1.1 maximum_bitcast_fusion.5
  63.2 1.1 maximum_bitcast_fusion.3
  64.4 62.7 %all-to-all-done.1 = f32[2,128,4,768]{3,2,0,1:T(4,128)S(1)} async-done(((f32[2,128,4,768]{3,2,0,1:T(4,128)}), f32[2,128,4,768]{3,2,0,1:T(4,128)S(1)}, u32[]{:S(2)}, u32[]{:S(2)}) %all-to-all-start.1) | async-done | bytes 3145760 | tf_op jit(solution)/shard_map/all_to_all | solution.py:116
  127.1 2.2 copy.57
  129.3 3.4 reshape.384
  132.7 6.6 %convolution_bitcast_fusion = f32[2,2,256,768]{3,2,1,0:T(8,128)S(1)} fusion(f32[2,2,256,768,1]{3,2,0,1,4:T(8,128)S(1)} %reshape.384, f32[1,2,256,256]{2,3,0,1:T(8,128)} %get-tuple-element.21, f32[1,2,256,256]{2,3,0,1:T(8,128)} %get-tuple-element.20), kind=kOutput, calls=%fused_computation.9 | convolution fusion | flops 4832100352 | bytes 7340032 | tf_op jit(solution)/shard_map/sfrc,strg->tfgc/dot_general | solution.py:45
  139.7 0.6 copy-done.3
  140.5 5.4 %fusion.3 = f32[2,2,256,768]{3,2,1,0:T(8,128)S(1)} fusion(f32[1,2,256,256]{3,2,1,0:T(8,128)S(1)} %get-tuple-element.13, f32[1,2,256,256]{3,2,1,0:T(8,128)S(1)} %get-tuple-element.12, f32[1,2,256,256]{3,2,1,0:T(8,128)S(1)} %get-tuple-element.10, f32[1,2,256,256]{3,2,1,0:T(8,128)S(1)} %get-tuple-element.9, f32[1,2,256,256]{3,2,1,0:T(8,128)S(1)} %get-tuple-element.11, ...), kind=kOutput, calls=%fused_computation.8 | convolution fusion | flops 4836032512 | bytes 7340032 | tf_op jit(solution)/shard_map/sfrc,strg->tfgc/dot_general | solution.py:45
  146.5 4.3 %copy.29 = f32[2,2,256,768]{3,1,0,2:T(2,128)} copy(f32[2,2,256,768]{3,2,1,0:T(8,128)S(1)} %pad_maximum_fusion.1) | data formatting | bytes 6291456 | tf_op jit(solution)/shard_map/stack | solution.py:18
  150.8 10.0 %all-to-all-start.2 = ((f32[2,2,256,768]{3,1,0,2:T(2,128)}), f32[2,2,256,768]{3,1,0,2:T(2,128)S(1)}, u32[]{:S(2)}, u32[]{:S(2)}) async-start(f32[2,2,256,768]{3,1,0,2:T(2,128)} %copy.29), calls=%async_computation.2 | async-start | bytes 6291456 | tf_op jit(solution)/shard_map/all_to_all | solution.py:121
  161.1 69.3 %all-to-all-done.2 = f32[2,2,256,768]{3,1,0,2:T(2,128)S(1)} async-done(((f32[2,2,256,768]{3,1,0,2:T(2,128)}), f32[2,2,256,768]{3,1,0,2:T(2,128)S(1)}, u32[]{:S(2)}, u32[]{:S(2)}) %all-to-all-start.2) | async-done | bytes 3145760 | tf_op jit(solution)/shard_map/all_to_all | solution.py:121
  230.4 2.8 copy.56
  233.2 3.9 %all_to_all.50 = f32[2,128,4,768]{3,1,0,2:T(8,128)S(1)} reshape(f32[2,64,2,4,768]{4,2,1,0,3:T(2,128)} %bitcast.75) | data formatting | bytes 6291456 | tf_op jit(solution)/shard_map/all_to_all | solution.py:121
  237.1 2.0 fusion.6
  239.7 30.4 %all_to_all.57 = f32[64,4,768]{2,1,0:T(4,128)S(1)} all-to-all(f32[64,4,768]{2,1,0:T(4,128)S(1)} %copy.31), channel_id=1, replica_groups=mesh['dp'=8,'seq'=64] {'seq'}, dimensions={0} | all-to-all | bytes 1572864 | tf_op jit(solution)/shard_map/all_to_all | solution.py:123
  270.4 0.9 fusion.20
  271.3 79.5 %all-reduce.2.cloned.1.call-done = f32[256,256]{1,0:T(8,128)} async-done(((f32[256,256]{1,0:T(8,128)}), f32[256,256]{1,0:T(8,128)}) %all-reduce.2.cloned.1.call-update) | async-done | bytes 262160 | tf_op jit(solution)/shard_map/psum | solution.py:127
  350.8 1.7 copy.60
  (31 shorter events, 4.9 us)
Async XLA Ops:
  13.4 29.8 %copy-start.5 = (f32[768]{0:T(1024)S(1)}, f32[768]{0:T(1024)}, u32[]{:S(2)}) copy-start(f32[768]{0:T(1024)} %constant.80.clone.1) | copy-start | bytes 9220
  14.4 26.0 %all-to-all-start = ((bf16[64,2,1536]{2,1,0:T(2,128)(2,1)}), bf16[64,2,1536]{2,1,0:T(2,128)(2,1)S(1)}, u32[]{:S(2)}, u32[]{:S(2)}) async-start(bf16[64,2,1536]{2,1,0:T(2,128)(2,1)} %reshape.393), calls=%async_computation | async-start | bytes 786432 | tf_op jit(solution)/shard_map/all_to_all | solution.py:110
  50.3 76.8 %all-to-all-start.1 = ((f32[2,128,4,768]{3,2,0,1:T(4,128)}), f32[2,128,4,768]{3,2,0,1:T(4,128)S(1)}, u32[]{:S(2)}, u32[]{:S(2)}) async-start(f32[2,128,4,768]{3,2,0,1:T(4,128)} %copy.25), calls=%async_computation.1 | async-start | bytes 6291456 | tf_op jit(solution)/shard_map/all_to_all | solution.py:116
  139.3 1.0 copy-start.3
  139.3 1.2 copy-start.4
  150.8 79.5 %all-to-all-start.2 = ((f32[2,2,256,768]{3,1,0,2:T(2,128)}), f32[2,2,256,768]{3,1,0,2:T(2,128)S(1)}, u32[]{:S(2)}, u32[]{:S(2)}) async-start(f32[2,2,256,768]{3,1,0,2:T(2,128)} %copy.29), calls=%async_computation.2 | async-start | bytes 6291456 | tf_op jit(solution)/shard_map/all_to_all | solution.py:121
  160.9 189.9 %all-reduce.2.cloned.1.call-start = ((), (), s32[]{:S(2)}) async-start(), calls=%async_computation.4 | async-start | bytes 524288 | tf_op jit(solution)/shard_map/psum | solution.py:127
  239.1 31.2 %copy-start = (bf16[1,256,256]{2,1,0:T(8,128)(2,1)S(1)}, bf16[1,256,256]{2,1,0:T(8,128)(2,1)}, u32[]{:S(2)}) copy-start(bf16[1,256,256]{2,1,0:T(8,128)(2,1)} %param.8) | copy-start | bytes 393220
  239.1 31.2 %copy-start.1 = (bf16[1,256,256]{2,1,0:T(8,128)(2,1)S(1)}, bf16[1,256,256]{2,1,0:T(8,128)(2,1)}, u32[]{:S(2)}) copy-start(bf16[1,256,256]{2,1,0:T(8,128)(2,1)} %param.7) | copy-start | bytes 393220
  239.1 31.2 %copy-start.2 = (bf16[1,256,256]{2,1,0:T(8,128)(2,1)S(1)}, bf16[1,256,256]{2,1,0:T(8,128)(2,1)}, u32[]{:S(2)}) copy-start(bf16[1,256,256]{2,1,0:T(8,128)(2,1)} %param.6) | copy-start | bytes 393220
Sparse Core Ops, SparseCore 0:
  271.4 79.3 all-reduce.1
where the time goes:
time: 364 us; the launch traced here: 360 us
  waiting for transfers between devices  224 us (62%)
  starting transfers between devices  31 us (9%)
  blocking collectives  30.4 us (8%)
  local copies, waits for them, and re-layouts  26.2 us (7%)
  matrix products  16.7 us (5%)
  other arithmetic  16.6 us (5%)
  between operations  14.6 us (4%)
    psum x1, waiting for transfers between devices, body(): grad_filter = lax.psum(filter_part[0] * scaling, 'dp')  79.5 us
    all_to_all x1, waiting for transfers between devices, body(): lax.all_to_all(back, 'seq', split_axis=2, concat_axis=1, tiled=True)  69.3 us
    all_to_all x1, waiting for transfers between devices, body(): moved = lax.all_to_all(half, 'seq', split_axis=1, concat_axis=2, tiled=True)  62.7 us
    all_to_all x1, blocking collectives, body(): lax.all_to_all(blocks, 'seq', split_axis=0, concat_axis=1, tiled=True)  30.4 us
    all_to_all x1, starting transfers between devices, body(): lax.all_to_all(combined, 'seq', split_axis=1, concat_axis=0, tiled=True)  13.2 us
    all_to_all x1, waiting for transfers between devices, body(): lax.all_to_all(combined, 'seq', split_axis=1, concat_axis=0, tiled=True)  12.5 us
    dot_general x2, matrix products, row_transform(): jnp.einsum('sfrc,strg->tfgc', paired, matrix, precision=highest_precision)  12 us
    all_to_all x1, starting transfers between devices, body(): lax.all_to_all(back, 'seq', split_axis=2, concat_axis=1, tiled=True)  10 us
  transfers between devices with their start and end apart: 4, of which 4 were waited for; matrix products, arithmetic and copies ran while one was open for 2% of the time, Pallas kernels for 0%

commit v1 on v0

v1 whole, which is shorter than its diff:
```python
import math

import jax
import jax.numpy as jnp
import numpy as np
from jax import lax
from jax.experimental import pallas as pl
from jax.experimental.pallas import tpu as pltpu
from jax.sharding import Mesh, PartitionSpec as P

HI, CORE, LO, Y, X = "hi", "core", "lo", "y", "x"
SIZES = (4, 2, 2, 8, 4)
SEQ_AXES = (LO, Y, X)
GROUP = (HI, LO, Y, X)
BLOCKS = 64
WIDTH = 256
ROWS = 64
LENGTH = 2 * BLOCKS * WIDTH


def split_bf16(array):
    high = array.astype(jnp.bfloat16)
    low = (array - high.astype(np.float32)).astype(jnp.bfloat16)
    return high, low


def tables():
    freq = np.arange(ROWS)[:, None] + 0.5
    block = np.arange(BLOCKS)[None, :]
    place = np.arange(WIDTH)
    angle = 2.0 * math.pi * freq * block / (2 * BLOCKS)
    enter = np.concatenate([np.cos(angle), -np.sin(angle)], axis=0).astype(np.float32)
    scale = 2.0 / LENGTH / math.sqrt(BLOCKS * WIDTH)
    leave = (scale * np.concatenate([np.cos(angle.T), -np.sin(angle.T)], axis=1)).astype(np.float32)
    turn = 2.0 * math.pi * freq * place[None, :] / LENGTH
    angle = 2.0 * math.pi * (place[:, None] * place[None, :] % WIDTH) / WIDTH
    cos_high, cos_low = split_bf16(np.cos(angle).astype(np.float32))
    sin_high, sin_low = split_bf16(np.sin(angle).astype(np.float32))
    return (
        np.concatenate(split_bf16(enter), axis=1),
        np.cos(turn).astype(np.float32),
        np.sin(turn).astype(np.float32),
        np.stack([cos_high, cos_low, sin_high, sin_low]),
        np.stack(split_bf16(leave)),
    )


def dot(left, right):
    return jnp.dot(left, right, preferred_element_type=jnp.float32)


def halves(array):
    high = array.astype(jnp.bfloat16)
    return high, (array - high.astype(jnp.float32)).astype(jnp.bfloat16)


def times_table(high, low, table_ref, at):
    return dot(high, table_ref[at]) + dot(low, table_ref[at]) + dot(high, table_ref[at + 1])


def convolve_kernel(x_ref, enter_ref, cos_ref, sin_ref, table_ref, leave_ref, out_ref):
    sequences = x_ref.shape[0] // BLOCKS
    turn_cos, turn_sin = cos_ref[...], sin_ref[...]
    signals = []
    for one in range(sequences):
        rows = slice(one * BLOCKS, (one + 1) * BLOCKS)
        signals += [x_ref[rows, :WIDTH], x_ref[rows, WIDTH : 2 * WIDTH]]
    signals.append(x_ref[:BLOCKS, 2 * WIDTH :])
    real_parts, imag_parts = [], []
    for signal in signals:
        first = dot(enter_ref[...], jnp.concatenate([signal, signal], axis=0))
        real, imag = first[:ROWS], first[ROWS:]
        real_parts.append(real * turn_cos + imag * turn_sin)
        imag_parts.append(imag * turn_cos - real * turn_sin)
    high, low = halves(jnp.concatenate(real_parts + imag_parts, axis=0))
    by_cos = times_table(high, low, table_ref, 0)
    by_sin = times_table(high, low, table_ref, 2)
    count = len(signals)
    half = count * ROWS
    spec_real = by_cos[:half] + by_sin[half:]
    spec_imag = by_cos[half:] - by_sin[:half]
    spectra = [
        (spec_real[i * ROWS : (i + 1) * ROWS], spec_imag[i * ROWS : (i + 1) * ROWS])
        for i in range(count)
    ]
    filt_real, filt_imag = spectra[-1]
    real_parts, imag_parts = [], []
    sum_real, sum_imag = None, None
    for one in range(sequences):
        mixed_real, mixed_imag = spectra[2 * one]
        gated_real, gated_imag = spectra[2 * one + 1]
        real_parts.append(mixed_real * filt_real - mixed_imag * filt_imag)
        imag_parts.append(mixed_real * filt_imag + mixed_imag * filt_real)
        real_parts.append(gated_real * filt_real + gated_imag * filt_imag)
        imag_parts.append(gated_imag * filt_real - gated_real * filt_imag)
        part_real = gated_real * mixed_real + gated_imag * mixed_imag
        part_imag = gated_imag * mixed_real - gated_real * mixed_imag
        sum_real = part_real if one == 0 else sum_real + part_real
        sum_imag = part_imag if one == 0 else sum_imag + part_imag
    real_parts.append(sum_real)
    imag_parts.append(sum_imag)
    high, low = halves(jnp.concatenate(real_parts + imag_parts, axis=0))
    by_cos = times_table(high, low, table_ref, 0)
    by_sin = times_table(high, low, table_ref, 2)
    back_real = by_cos[:half] - by_sin[half:]
    back_imag = by_cos[half:] + by_sin[:half]
    results = []
    for i in range(count):
        real = back_real[i * ROWS : (i + 1) * ROWS]
        imag = back_imag[i * ROWS : (i + 1) * ROWS]
        turned = jnp.concatenate(
            [real * turn_cos - imag * turn_sin, imag * turn_cos + real * turn_sin], axis=0
        )
        high, low = halves(turned)
        value = dot(leave_ref[0], high) + dot(leave_ref[0], low) + dot(leave_ref[1], high)
        results.append(value.astype(jnp.bfloat16))
    for one in range(sequences):
        rows = slice(one * BLOCKS, (one + 1) * BLOCKS)
        out_ref[rows, :WIDTH] = results[2 * one]
        out_ref[rows, WIDTH : 2 * WIDTH] = results[2 * one + 1]
        out_ref[rows, 2 * WIDTH :] = results[-1]


def convolve(rows_in):
    return pl.pallas_call(
        convolve_kernel,
        out_shape=jax.ShapeDtypeStruct(rows_in.shape, jnp.bfloat16),
        in_specs=[pl.BlockSpec(memory_space=pltpu.VMEM)] * 6,
        out_specs=pl.BlockSpec(memory_space=pltpu.VMEM),
        compiler_params=pltpu.CompilerParams(vmem_limit_bytes=32 * 1024 * 1024),
        name="convolve",
    )(rows_in, *(jnp.asarray(t) for t in tables()))


def exchange(rows):
    count, width = rows.shape
    moved = lax.all_to_all(
        rows.reshape(count, 2, width // 2), GROUP, split_axis=0, concat_axis=0, tiled=True
    )
    return moved.reshape(count, width)


def body(query_gate, key_gate, values_in, grad_out, long_filter):
    key_wide = key_gate[0].astype(jnp.float32)
    values_wide = values_in[0].astype(jnp.float32)
    grad_wide = grad_out[0].astype(jnp.float32)
    mixed_in = (key_wide * values_wide).astype(jnp.bfloat16)
    gated_grad = (grad_wide * query_gate[0].astype(jnp.float32)).astype(jnp.bfloat16)
    packed = jnp.concatenate([mixed_in.T, gated_grad.T, long_filter.T], axis=1)
    moved = exchange(packed)
    result = convolve(moved)
    returned = exchange(result)
    part = returned[:, 2 * WIDTH :]
    other = lax.ppermute(part, CORE, [(0, 1), (1, 0)])
    conv_out = returned[:, :WIDTH].T.astype(jnp.float32)
    grad_mixed = returned[:, WIDTH : 2 * WIDTH].T.astype(jnp.float32)
    grad_query = (grad_wide * conv_out).astype(jnp.bfloat16)
    grad_key = (grad_mixed * values_wide).astype(jnp.bfloat16)
    grad_value = (grad_mixed * key_wide).astype(jnp.bfloat16)
    grad_filter = (part.astype(jnp.float32) + other.astype(jnp.float32)).T
    return (grad_query[None], grad_key[None], grad_value[None], grad_filter)


def solution(mesh):
    fine = Mesh(mesh.devices.reshape(SIZES), (HI, CORE, LO, Y, X))
    whole = P((HI, CORE), SEQ_AXES, None)
    return jax.shard_map(
        body,
        mesh=fine,
        in_specs=(whole, whole, whole, whole, P(SEQ_AXES, None)),
        out_specs=(whole, whole, whole, P(SEQ_AXES, None)),
        check_vma=False,
    )
```

time: 364 us -> 79.7 us (0.22); the launches traced: 360 us -> 79.5 us
  waiting for transfers between devices: 224 us -> 0.11 us
  blocking collectives: 30.4 us -> 63.3 us
  starting transfers between devices: 31 us -> 5.84 us
  local copies, waits for them, and re-layouts: 26.2 us -> 2.13 us
  matrix products: 16.7 us -> 0 us
  between operations: 14.6 us -> 0.77 us
  other arithmetic: 16.6 us -> 2.79 us
  Pallas kernels: 0 us -> 4.5 us
    all_to_all x3 -> x0, waiting for transfers between devices: 145 us -> none  [the longest x1 69.3 us: body(): lax.all_to_all(back, 'seq', split_axis=2, concat_axis=1, tiled=True)]
    psum x1 -> x0, waiting for transfers between devices: 79.5 us -> none  [body(): grad_filter = lax.psum(filter_part[0] * scaling, 'dp')]
    all_to_all x1 -> x2, blocking collectives: 30.4 us -> 63.3 us  [exchange(): lax.all_to_all(rows.reshape(count, 2, width // 2), GROUP, split_axis=0, c...]
    all_to_all x3 -> x0, starting transfers between devices: 31 us -> none  [the longest x1 13.2 us: body(): lax.all_to_all(combined, 'seq', split_axis=1, concat_axis=0, tiled=True)]
    dot_general x4 -> x0, matrix products: 16.7 us -> none  [the longest x2 12 us: row_transform(): jnp.einsum('sfrc,strg->tfgc', paired, matrix, precision=highest_precision)]
    all_to_all x5 -> x1, local copies, waits for them, and re-layouts: 12.6 us -> 0.48 us  [exchange(): lax.all_to_all(rows.reshape(count, 2, width // 2), GROUP, split_axis=0, c...]
    another operation x2 -> x0, local copies, waits for them, and re-layouts: 7.97 us -> none  [twist(): jnp.stack([paired[0] * cosine - paired[1] * sine_part, paired[0] * sine_p...]
    ppermute x0 -> x1, starting transfers between devices: none -> 5.84 us  [body(): other = lax.ppermute(part, CORE, [(0, 1), (1, 0)])]
  transfers between devices with their start and end apart: 4 -> 1, of which waited for: 4 -> 1; matrix products, arithmetic and copies ran while one was open for 2% -> 1% of each run, Pallas kernels for 0% -> 0%
where the time goes in v1:
time: 79.7 us; the launch traced here: 79.5 us
  blocking collectives  63.3 us (79%)
  starting transfers between devices  5.84 us (7%)
  Pallas kernels  4.5 us (6%)
  other arithmetic  2.79 us (4%)
  local copies, waits for them, and re-layouts  2.13 us (3%)
    all_to_all x2, blocking collectives, exchange(): lax.all_to_all(rows.reshape(count, 2, width // 2), GROUP, split_axis=0, c...  63.3 us
    ppermute x1, starting transfers between devices, body(): other = lax.ppermute(part, CORE, [(0, 1), (1, 0)])  5.84 us
    pallas_call x1, Pallas kernels, convolve(): pl.pallas_call(convolve_kernel, out_shape=jax.ShapeDtypeStruct(rows_in.sh...  4.5 us
  transfers between devices with their start and end apart: 1, of which 1 were waited for; matrix products, arithmetic and copies ran while one was open for 1% of the time, Pallas kernels for 0%

profile of v1, /device:TPU:1, one launch (start us, length us, event | category | flops | bytes accessed | tf_op | source)
XLA Modules:
  0.0 79.5 jit_solution(2353260413422546601)
XLA Ops:
  0.6 0.0 copy-start.8
  0.6 1.2 %fusion.6 = (bf16[256,256]{0,1:T(8,128)(2,1)S(1)}, bf16[256,256]{0,1:T(8,128)(2,1)S(1)}) fusion(bf16[1,256,256]{2,1,0:T(8,128)(2,1)} %param.11, bf16[1,256,256]{2,1,0:T(8,128)(2,1)} %param.12, bf16[1,256,256]{2,1,0:T(8,128)(2,1)} %param.10, bf16[1,256,256]{2,1,0:T(8,128)(2,1)} %param.13), kind=kLoop, calls=%fused_computation.13 | loop fusion | flops 524288 | bytes 786432 | tf_op jit(solution)/shard_map/transpose | solution.py:149
  1.8 0.0 copy-done.8
  1.9 0.5 copy.14
  2.4 38.3 %all_to_all.10 = bf16[256,2,384]{2,1,0:T(2,128)(2,1)S(1)} all-to-all(bf16[256,2,384]{2,1,0:T(2,128)(2,1)S(1)} %copy.14), channel_id=1, replica_groups=mesh['hi'=4,'core'=2,'lo'=2,'y'=8,'x'=4] {'hi','lo','y','x'}, dimensions={0} | all-to-all | bytes 786432 | tf_op jit(solution)/shard_map/all_to_all | solution.py:137
  40.6 0.0 copy-start
  40.6 0.0 copy-start.1
  40.6 0.0 copy-start.2
  40.6 0.0 copy-start.3
  40.6 0.0 copy-start.4
  40.7 0.1 copy.16
  40.7 1.0 %copy-done = bf16[4,256,256]{2,1,0:T(8,128)(2,1)S(1)} copy-done((bf16[4,256,256]{2,1,0:T(8,128)(2,1)S(1)}, bf16[4,256,256]{2,1,0:T(8,128)(2,1)}, u32[]{:S(2)}) %copy-start) | copy-done | bytes 524312
  41.7 0.0 copy-done.1
  41.7 0.0 copy-done.2
  41.7 0.0 copy-done.3
  41.7 0.0 copy-done.4
  41.7 4.5 %convolve.1 = bf16[256,768]{1,0:T(8,128)(2,1)S(1)} custom-call(bf16[256,768]{1,0:T(8,128)(2,1)S(1)} %bitcast.43, bf16[128,128]{1,0:T(8,128)(2,1)S(1)} %copy-done.4, f32[64,256]{1,0:T(8,128)S(1)} %copy-done.2, f32[64,256]{1,0:T(8,128)S(1)} %copy-done.1, bf16[4,256,256]{2,1,0:T(8,128)(2,1)S(1)} %copy-done, bf16[2,64,128]{2,1,0:T(8,128)(2,1)S(1)} %copy-done.3), custom_call_target="tpu_custom_call" | custom-call | tf_op jit(solution)/shard_map/convolve/pallas_call | solution.py:125
  46.2 0.1 reshape.30
  46.3 25.1 %all_to_all.11 = bf16[256,2,384]{2,1,0:T(2,128)(2,1)S(1)} all-to-all(bf16[256,2,384]{2,1,0:T(2,128)(2,1)S(1)} %reshape.30), channel_id=1, replica_groups=mesh['hi'=4,'core'=2,'lo'=2,'y'=8,'x'=4] {'hi','lo','y','x'}, dimensions={0} | all-to-all | bytes 786432 | tf_op jit(solution)/shard_map/all_to_all | solution.py:137
  71.4 0.0 copy-start.7
  71.4 0.5 copy.15
  71.9 0.0 copy-start.5
  71.9 0.0 copy-start.6
  71.9 5.8 %collective-permute-start = (bf16[256,256]{0,1:T(8,128)(2,1)S(1)}, bf16[256,256]{0,1:T(8,128)(2,1)S(1)}, u32[]{:S(2)}, u32[]{:S(2)}) collective-permute-start(bf16[256,256]{0,1:T(8,128)(2,1)S(1)} %slice.14), channel_id=1, source_target_pairs={{0,64},{64,0},{1,65},{65,1},{2,66},{66,2},{3,67},{67,3},{4,68},{68... | collective-permute-start | bytes 393224 | tf_op jit(solution)/shard_map/ppermute | solution.py:154
  77.8 0.0 copy-done.7
  77.8 0.0 copy-done.5
  77.8 0.0 copy-done.6
  77.8 0.8 %fusion.5 = (bf16[1,256,256]{2,1,0:T(8,128)(2,1)}, bf16[1,256,256]{2,1,0:T(8,128)(2,1)}, bf16[1,256,256]{2,1,0:T(8,128)(2,1)}) fusion(bf16[1,256,256]{2,1,0:T(8,128)(2,1)S(1)} %copy-done.5, bf16[256,768]{0,1:T(8,128)(2,1)S(1)} %bitcast.45, bf16[1,256,256]{2,1,0:T(8,128)(2,1)S(1)} %copy-done.6, bf16[1,256,256]{2,1,0:T(8,128)(2,1)S(1)} %copy-done.7), kind=kLoop, calls=%fused_computation.12 | loop fusion | flops 720896 | bytes 1048576 | tf_op jit(solution)/shard_map/broadcast_in_dim | solution.py:161
  78.6 0.1 collective-permute-done
  78.7 0.7 add_bitcast_fusion
  (2 shorter events, 0.0 us)
Async XLA Ops:
  0.6 1.2 %copy-start.8 = (bf16[256,256]{1,0:T(8,128)(2,1)S(1)}, bf16[256,256]{1,0:T(8,128)(2,1)}, u32[]{:S(2)}) copy-start(bf16[256,256]{1,0:T(8,128)(2,1)} %param.14) | copy-start | bytes 393220
  40.6 1.0 %copy-start = (bf16[4,256,256]{2,1,0:T(8,128)(2,1)S(1)}, bf16[4,256,256]{2,1,0:T(8,128)(2,1)}, u32[]{:S(2)}) copy-start(bf16[4,256,256]{2,1,0:T(8,128)(2,1)} %constant.13.clone.table_ref) | copy-start | bytes 1572868
  40.6 1.0 %copy-start.1 = (f32[64,256]{1,0:T(8,128)S(1)}, f32[64,256]{1,0:T(8,128)}, u32[]{:S(2)}) copy-start(f32[64,256]{1,0:T(8,128)} %constant.12.clone.sin_ref) | copy-start | bytes 196612
  40.6 1.0 %copy-start.2 = (f32[64,256]{1,0:T(8,128)S(1)}, f32[64,256]{1,0:T(8,128)}, u32[]{:S(2)}) copy-start(f32[64,256]{1,0:T(8,128)} %constant.11.clone.cos_ref) | copy-start | bytes 196612
  40.6 1.0 %copy-start.3 = (bf16[2,64,128]{2,1,0:T(8,128)(2,1)S(1)}, bf16[2,64,128]{2,1,0:T(8,128)(2,1)}, u32[]{:S(2)}) copy-start(bf16[2,64,128]{2,1,0:T(8,128)(2,1)} %constant.14.clone.leave_ref) | copy-start | bytes 98308
  40.6 1.0 %copy-start.4 = (bf16[128,128]{1,0:T(8,128)(2,1)S(1)}, bf16[128,128]{1,0:T(8,128)(2,1)}, u32[]{:S(2)}) copy-start(bf16[128,128]{1,0:T(8,128)(2,1)} %constant.10.clone.enter_ref) | copy-start | bytes 98308
  71.4 6.4 %copy-start.7 = (bf16[1,256,256]{2,1,0:T(8,128)(2,1)S(1)}, bf16[1,256,256]{2,1,0:T(8,128)(2,1)}, u32[]{:S(2)}) copy-start(bf16[1,256,256]{2,1,0:T(8,128)(2,1)} %param.13) | copy-start | bytes 393220
  71.9 5.9 %copy-start.5 = (bf16[1,256,256]{2,1,0:T(8,128)(2,1)S(1)}, bf16[1,256,256]{2,1,0:T(8,128)(2,1)}, u32[]{:S(2)}) copy-start(bf16[1,256,256]{2,1,0:T(8,128)(2,1)} %param.11) | copy-start | bytes 393220
  71.9 5.9 %copy-start.6 = (bf16[1,256,256]{2,1,0:T(8,128)(2,1)S(1)}, bf16[1,256,256]{2,1,0:T(8,128)(2,1)}, u32[]{:S(2)}) copy-start(bf16[1,256,256]{2,1,0:T(8,128)(2,1)} %param.12) | copy-start | bytes 393220
  71.9 6.8 %collective-permute-start = (bf16[256,256]{0,1:T(8,128)(2,1)S(1)}, bf16[256,256]{0,1:T(8,128)(2,1)S(1)}, u32[]{:S(2)}, u32[]{:S(2)}) collective-permute-start(bf16[256,256]{0,1:T(8,128)(2,1)S(1)} %slice.14), channel_id=1, source_target_pairs={{0,64},{64,0},{1,65},{65,1},{2,66},{66,2},{3,67},{67,3},{4,68},{68... | collective-permute-start | bytes 393224 | tf_op jit(solution)/shard_map/ppermute | solution.py:154

commit v2 on v1

--- a/solution.py
+++ b/solution.py
@@ -36,12 +36,13 @@
     angle = 2.0 * math.pi * (place[:, None] * place[None, :] % WIDTH) / WIDTH
     cos_high, cos_low = split_bf16(np.cos(angle).astype(np.float32))
     sin_high, sin_low = split_bf16(np.sin(angle).astype(np.float32))
+    leave_high, leave_low = split_bf16(leave)
     return (
         np.concatenate(split_bf16(enter), axis=1),
         np.cos(turn).astype(np.float32),
         np.sin(turn).astype(np.float32),
         np.stack([cos_high, cos_low, sin_high, sin_low]),
-        np.stack(split_bf16(leave)),
+        np.concatenate([leave_high, leave_high, leave_low], axis=1),
     )
 
 
@@ -54,8 +55,18 @@
     return high, (array - high.astype(jnp.float32)).astype(jnp.bfloat16)
 
 
-def times_table(high, low, table_ref, at):
-    return dot(high, table_ref[at]) + dot(low, table_ref[at]) + dot(high, table_ref[at + 1])
+def turn_by(parts, high_table, low_table):
+    high, low = halves(parts)
+    return dot(
+        jnp.concatenate([high, low, high], axis=1),
+        jnp.concatenate([high_table, high_table, low_table], axis=0),
+    )
+
+
+def complex_table(cosine, sine):
+    return jnp.concatenate(
+        [jnp.concatenate([cosine, sine], axis=1), jnp.concatenate([-sine, cosine], axis=1)], axis=0
+    )
 
 
 def convolve_kernel(x_ref, enter_ref, cos_ref, sin_ref, table_ref, leave_ref, out_ref):
@@ -66,59 +77,81 @@
         rows = slice(one * BLOCKS, (one + 1) * BLOCKS)
         signals += [x_ref[rows, :WIDTH], x_ref[rows, WIDTH : 2 * WIDTH]]
     signals.append(x_ref[:BLOCKS, 2 * WIDTH :])
-    real_parts, imag_parts = [], []
-    for signal in signals:
-        first = dot(enter_ref[...], jnp.concatenate([signal, signal], axis=0))
-        real, imag = first[:ROWS], first[ROWS:]
-        real_parts.append(real * turn_cos + imag * turn_sin)
-        imag_parts.append(imag * turn_cos - real * turn_sin)
-    high, low = halves(jnp.concatenate(real_parts + imag_parts, axis=0))
-    by_cos = times_table(high, low, table_ref, 0)
-    by_sin = times_table(high, low, table_ref, 2)
     count = len(signals)
-    half = count * ROWS
-    spec_real = by_cos[:half] + by_sin[half:]
-    spec_imag = by_cos[half:] - by_sin[:half]
-    spectra = [
-        (spec_real[i * ROWS : (i + 1) * ROWS], spec_imag[i * ROWS : (i + 1) * ROWS])
-        for i in range(count)
-    ]
-    filt_real, filt_imag = spectra[-1]
-    real_parts, imag_parts = [], []
-    sum_real, sum_imag = None, None
+    signals = jnp.concatenate(signals, axis=1)
+    first = dot(enter_ref[...], jnp.concatenate([signals, signals], axis=0))
+    parts = []
+    for i in range(count):
+        real = first[:ROWS, i * WIDTH : (i + 1) * WIDTH]
+        imag = first[ROWS:, i * WIDTH : (i + 1) * WIDTH]
+        parts.append(
+            jnp.concatenate(
+                [real * turn_cos + imag * turn_sin, imag * turn_cos - real * turn_sin], axis=1
+            )
+        )
+    spectra = turn_by(
+        jnp.concatenate(parts, axis=0),
+        complex_table(table_ref[0], -table_ref[2]),
+        complex_table(table_ref[1], -table_ref[3]),
+    )
+
+    def spectrum(i):
+        rows = slice(i * ROWS, (i + 1) * ROWS)
+        return spectra[rows, :WIDTH], spectra[rows, WIDTH:]
+
+    filt_real, filt_imag = spectrum(count - 1)
+    parts = []
+    total = None
     for one in range(sequences):
-        mixed_real, mixed_imag = spectra[2 * one]
-        gated_real, gated_imag = spectra[2 * one + 1]
-        real_parts.append(mixed_real * filt_real - mixed_imag * filt_imag)
-        imag_parts.append(mixed_real * filt_imag + mixed_imag * filt_real)
-        real_parts.append(gated_real * filt_real + gated_imag * filt_imag)
-        imag_parts.append(gated_imag * filt_real - gated_real * filt_imag)
-        part_real = gated_real * mixed_real + gated_imag * mixed_imag
-        part_imag = gated_imag * mixed_real - gated_real * mixed_imag
-        sum_real = part_real if one == 0 else sum_real + part_real
-        sum_imag = part_imag if one == 0 else sum_imag + part_imag
-    real_parts.append(sum_real)
-    imag_parts.append(sum_imag)
-    high, low = halves(jnp.concatenate(real_parts + imag_parts, axis=0))
-    by_cos = times_table(high, low, table_ref, 0)
-    by_sin = times_table(high, low, table_ref, 2)
-    back_real = by_cos[:half] - by_sin[half:]
-    back_imag = by_cos[half:] + by_sin[:half]
-    results = []
+        mixed_real, mixed_imag = spectrum(2 * one)
+        gated_real, gated_imag = spectrum(2 * one + 1)
+        parts.append(
+            jnp.concatenate(
+                [
+                    mixed_real * filt_real - mixed_imag * filt_imag,
+                    mixed_real * filt_imag + mixed_imag * filt_real,
+                ],
+                axis=1,
+            )
+        )
+        parts.append(
+            jnp.concatenate(
+                [
+                    gated_real * filt_real + gated_imag * filt_imag,
+                    gated_imag * filt_real - gated_real * filt_imag,
+                ],
+                axis=1,
+            )
+        )
+        part = jnp.concatenate(
+            [
+                gated_real * mixed_real + gated_imag * mixed_imag,
+                gated_imag * mixed_real - gated_real * mixed_imag,
+            ],
+            axis=1,
+        )
+        total = part if one == 0 else total + part
+    parts.append(total)
+    back = turn_by(
+        jnp.concatenate(parts, axis=0),
+        complex_table(table_ref[0], table_ref[2]),
+        complex_table(table_ref[1], table_ref[3]),
+    )
+    turned = []
     for i in range(count):
-        real = back_real[i * ROWS : (i + 1) * ROWS]
-        imag = back_imag[i * ROWS : (i + 1) * ROWS]
-        turned = jnp.concatenate(
-            [real * turn_cos - imag * turn_sin, imag * turn_cos + real * turn_sin], axis=0
-        )
-        high, low = halves(turned)
-        value = dot(leave_ref[0], high) + dot(leave_ref[0], low) + dot(leave_ref[1], high)
-        results.append(value.astype(jnp.bfloat16))
+        real = back[i * ROWS : (i + 1) * ROWS, :WIDTH]
+        imag = back[i * ROWS : (i + 1) * ROWS, WIDTH:]
+        turned.append(
+            jnp.concatenate(
+                [real * turn_cos - imag * turn_sin, imag * turn_cos + real * turn_sin], axis=0
+            )
+        )
+    high, low = halves(jnp.concatenate(turned, axis=1))
+    values = dot(leave_ref[...], jnp.concatenate([high, low, high], axis=0)).astype(jnp.bfloat16)
     for one in range(sequences):
         rows = slice(one * BLOCKS, (one + 1) * BLOCKS)
-        out_ref[rows, :WIDTH] = results[2 * one]
-        out_ref[rows, WIDTH : 2 * WIDTH] = results[2 * one + 1]
-        out_ref[rows, 2 * WIDTH :] = results[-1]
+        out_ref[rows, : 2 * WIDTH] = values[:, 2 * one * WIDTH : 2 * (one + 1) * WIDTH]
+        out_ref[rows, 2 * WIDTH :] = values[:, (count - 1) * WIDTH :]
 
 
 def convolve(rows_in):

time: 79.7 us -> 77.9 us (0.977)
  Pallas kernels: 4.5 us -> 2.69 us
    pallas_call x1, Pallas kernels: 4.5 us -> 2.69 us  [convolve(): pl.pallas_call(convolve_kernel, out_shape=jax.ShapeDtypeStruct(rows_in.sh...]
where the time goes in v2:
time: 77.9 us; the launch traced here: 77.7 us
  blocking collectives  63.4 us (81%)
  starting transfers between devices  5.82 us (7%)
  other arithmetic  2.79 us (4%)
  Pallas kernels  2.69 us (3%)
  local copies, waits for them, and re-layouts  2.13 us (3%)
    all_to_all x2, blocking collectives, exchange(): lax.all_to_all(rows.reshape(count, 2, width // 2), GROUP, split_axis=0, c...  63.4 us
    ppermute x1, starting transfers between devices, body(): other = lax.ppermute(part, CORE, [(0, 1), (1, 0)])  5.82 us
    pallas_call x1, Pallas kernels, convolve(): pl.pallas_call(convolve_kernel, out_shape=jax.ShapeDtypeStruct(rows_in.sh...  2.69 us
  transfers between devices with their start and end apart: 1, of which 1 were waited for; matrix products, arithmetic and copies ran while one was open for 1% of the time, Pallas kernels for 0%

profile of v2, /device:TPU:1, one launch (start us, length us, event | category | flops | bytes accessed | tf_op | source)
XLA Modules:
  0.0 77.7 jit_solution(16130005069252472703)
XLA Ops:
  0.6 0.0 copy-start.8
  0.6 1.2 %fusion.6 = (bf16[256,256]{0,1:T(8,128)(2,1)S(1)}, bf16[256,256]{0,1:T(8,128)(2,1)S(1)}) fusion(bf16[1,256,256]{2,1,0:T(8,128)(2,1)} %param.11, bf16[1,256,256]{2,1,0:T(8,128)(2,1)} %param.12, bf16[1,256,256]{2,1,0:T(8,128)(2,1)} %param.10, bf16[1,256,256]{2,1,0:T(8,128)(2,1)} %param.13), kind=kLoop, calls=%fused_computation.13 | loop fusion | flops 524288 | bytes 786432 | tf_op jit(solution)/shard_map/transpose | solution.py:182
  1.8 0.0 copy-done.8
  1.9 0.5 copy.14
  2.4 38.3 %all_to_all.10 = bf16[256,2,384]{2,1,0:T(2,128)(2,1)S(1)} all-to-all(bf16[256,2,384]{2,1,0:T(2,128)(2,1)S(1)} %copy.14), channel_id=1, replica_groups=mesh['hi'=4,'core'=2,'lo'=2,'y'=8,'x'=4] {'hi','lo','y','x'}, dimensions={0} | all-to-all | bytes 786432 | tf_op jit(solution)/shard_map/all_to_all | solution.py:170
  40.6 0.0 copy-start
  40.6 0.0 copy-start.1
  40.6 0.0 copy-start.2
  40.6 0.0 copy-start.3
  40.6 0.0 copy-start.4
  40.7 0.1 copy.16
  40.7 1.0 %copy-done = bf16[4,256,256]{2,1,0:T(8,128)(2,1)S(1)} copy-done((bf16[4,256,256]{2,1,0:T(8,128)(2,1)S(1)}, bf16[4,256,256]{2,1,0:T(8,128)(2,1)}, u32[]{:S(2)}) %copy-start) | copy-done | bytes 524312
  41.7 0.0 copy-done.1
  41.7 0.0 copy-done.2
  41.7 0.0 copy-done.3
  41.7 0.0 copy-done.4
  41.7 2.7 %convolve.1 = bf16[256,768]{1,0:T(8,128)(2,1)S(1)} custom-call(bf16[256,768]{1,0:T(8,128)(2,1)S(1)} %bitcast.43, bf16[128,128]{1,0:T(8,128)(2,1)S(1)} %copy-done.4, f32[64,256]{1,0:T(8,128)S(1)} %copy-done.2, f32[64,256]{1,0:T(8,128)S(1)} %copy-done.1, bf16[4,256,256]{2,1,0:T(8,128)(2,1)S(1)} %copy-done, bf16[64,384]{1,0:T(8,128)(2,1)S(1)} %copy-done.3), custom_call_target="tpu_custom_call" | custom-call | tf_op jit(solution)/shard_map/convolve/pallas_call | solution.py:158
  44.4 0.1 reshape.30
  44.5 25.1 %all_to_all.11 = bf16[256,2,384]{2,1,0:T(2,128)(2,1)S(1)} all-to-all(bf16[256,2,384]{2,1,0:T(2,128)(2,1)S(1)} %reshape.30), channel_id=1, replica_groups=mesh['hi'=4,'core'=2,'lo'=2,'y'=8,'x'=4] {'hi','lo','y','x'}, dimensions={0} | all-to-all | bytes 786432 | tf_op jit(solution)/shard_map/all_to_all | solution.py:170
  69.6 0.0 copy-start.7
  69.6 0.5 copy.15
  70.1 0.0 copy-start.5
  70.1 0.0 copy-start.6
  70.1 5.8 %collective-permute-start = (bf16[256,256]{0,1:T(8,128)(2,1)S(1)}, bf16[256,256]{0,1:T(8,128)(2,1)S(1)}, u32[]{:S(2)}, u32[]{:S(2)}) collective-permute-start(bf16[256,256]{0,1:T(8,128)(2,1)S(1)} %slice.14), channel_id=1, source_target_pairs={{0,64},{64,0},{1,65},{65,1},{2,66},{66,2},{3,67},{67,3},{4,68},{68... | collective-permute-start | bytes 393224 | tf_op jit(solution)/shard_map/ppermute | solution.py:187
  76.0 0.0 copy-done.7
  76.0 0.0 copy-done.5
  76.0 0.0 copy-done.6
  76.0 0.8 %fusion.5 = (bf16[1,256,256]{2,1,0:T(8,128)(2,1)}, bf16[1,256,256]{2,1,0:T(8,128)(2,1)}, bf16[1,256,256]{2,1,0:T(8,128)(2,1)}) fusion(bf16[1,256,256]{2,1,0:T(8,128)(2,1)S(1)} %copy-done.5, bf16[256,768]{0,1:T(8,128)(2,1)S(1)} %bitcast.45, bf16[1,256,256]{2,1,0:T(8,128)(2,1)S(1)} %copy-done.6, bf16[1,256,256]{2,1,0:T(8,128)(2,1)S(1)} %copy-done.7), kind=kLoop, calls=%fused_computation.12 | loop fusion | flops 720896 | bytes 1048576 | tf_op jit(solution)/shard_map/broadcast_in_dim | solution.py:194
  76.8 0.1 collective-permute-done
  76.9 0.7 add_bitcast_fusion
  (2 shorter events, 0.0 us)
Async XLA Ops:
  0.6 1.2 %copy-start.8 = (bf16[256,256]{1,0:T(8,128)(2,1)S(1)}, bf16[256,256]{1,0:T(8,128)(2,1)}, u32[]{:S(2)}) copy-start(bf16[256,256]{1,0:T(8,128)(2,1)} %param.14) | copy-start | bytes 393220
  40.6 1.0 %copy-start = (bf16[4,256,256]{2,1,0:T(8,128)(2,1)S(1)}, bf16[4,256,256]{2,1,0:T(8,128)(2,1)}, u32[]{:S(2)}) copy-start(bf16[4,256,256]{2,1,0:T(8,128)(2,1)} %constant.13.clone.table_ref) | copy-start | bytes 1572868
  40.6 1.0 %copy-start.1 = (f32[64,256]{1,0:T(8,128)S(1)}, f32[64,256]{1,0:T(8,128)}, u32[]{:S(2)}) copy-start(f32[64,256]{1,0:T(8,128)} %constant.12.clone.sin_ref) | copy-start | bytes 196612
  40.6 1.0 %copy-start.2 = (f32[64,256]{1,0:T(8,128)S(1)}, f32[64,256]{1,0:T(8,128)}, u32[]{:S(2)}) copy-start(f32[64,256]{1,0:T(8,128)} %constant.11.clone.cos_ref) | copy-start | bytes 196612
  40.6 1.0 %copy-start.3 = (bf16[64,384]{1,0:T(8,128)(2,1)S(1)}, bf16[64,384]{1,0:T(8,128)(2,1)}, u32[]{:S(2)}) copy-start(bf16[64,384]{1,0:T(8,128)(2,1)} %constant.14.clone.leave_ref) | copy-start | bytes 147460
  40.6 1.0 %copy-start.4 = (bf16[128,128]{1,0:T(8,128)(2,1)S(1)}, bf16[128,128]{1,0:T(8,128)(2,1)}, u32[]{:S(2)}) copy-start(bf16[128,128]{1,0:T(8,128)(2,1)} %constant.10.clone.enter_ref) | copy-start | bytes 98308
  69.6 6.4 %copy-start.7 = (bf16[1,256,256]{2,1,0:T(8,128)(2,1)S(1)}, bf16[1,256,256]{2,1,0:T(8,128)(2,1)}, u32[]{:S(2)}) copy-start(bf16[1,256,256]{2,1,0:T(8,128)(2,1)} %param.13) | copy-start | bytes 393220
  70.1 5.9 %copy-start.5 = (bf16[1,256,256]{2,1,0:T(8,128)(2,1)S(1)}, bf16[1,256,256]{2,1,0:T(8,128)(2,1)}, u32[]{:S(2)}) copy-start(bf16[1,256,256]{2,1,0:T(8,128)(2,1)} %param.11) | copy-start | bytes 393220
  70.1 5.9 %copy-start.6 = (bf16[1,256,256]{2,1,0:T(8,128)(2,1)S(1)}, bf16[1,256,256]{2,1,0:T(8,128)(2,1)}, u32[]{:S(2)}) copy-start(bf16[1,256,256]{2,1,0:T(8,128)(2,1)} %param.12) | copy-start | bytes 393220
  70.1 6.8 %collective-permute-start = (bf16[256,256]{0,1:T(8,128)(2,1)S(1)}, bf16[256,256]{0,1:T(8,128)(2,1)S(1)}, u32[]{:S(2)}, u32[]{:S(2)}) collective-permute-start(bf16[256,256]{0,1:T(8,128)(2,1)S(1)} %slice.14), channel_id=1, source_target_pairs={{0,64},{64,0},{1,65},{65,1},{2,66},{66,2},{3,67},{67,3},{4,68},{68... | collective-permute-start | bytes 393224 | tf_op jit(solution)/shard_map/ppermute | solution.py:187

commit v3 on v2

--- a/solution.py
+++ b/solution.py
@@ -36,14 +36,20 @@
     angle = 2.0 * math.pi * (place[:, None] * place[None, :] % WIDTH) / WIDTH
     cos_high, cos_low = split_bf16(np.cos(angle).astype(np.float32))
     sin_high, sin_low = split_bf16(np.sin(angle).astype(np.float32))
-    leave_high, leave_low = split_bf16(leave)
-    return (
-        np.concatenate(split_bf16(enter), axis=1),
-        np.cos(turn).astype(np.float32),
-        np.sin(turn).astype(np.float32),
-        np.stack([cos_high, cos_low, sin_high, sin_low]),
-        np.concatenate([leave_high, leave_high, leave_low], axis=1),
-    )
+    enter = np.concatenate(split_bf16(enter), axis=1)
+    coarse = np.concatenate(
+        [
+            cos_high[: WIDTH // 2],
+            cos_low[: WIDTH // 2],
+            sin_high[: WIDTH // 2],
+            sin_low[: WIDTH // 2],
+            np.pad(enter, ((0, 0), (0, WIDTH - enter.shape[1]))),
+            np.concatenate(split_bf16(leave), axis=1),
+        ],
+        axis=0,
+    )
+    fine = np.concatenate([np.cos(turn), np.sin(turn)], axis=0).astype(np.float32)
+    return coarse, fine
 
 
 def dot(left, right):
@@ -69,9 +75,17 @@
     )
 
 
-def convolve_kernel(x_ref, enter_ref, cos_ref, sin_ref, table_ref, leave_ref, out_ref):
+def convolve_kernel(x_ref, coarse_ref, fine_ref, out_ref):
+    cos_high, cos_low, sin_high, sin_low = (
+        coarse_ref[i * WIDTH : (i + 1) * WIDTH] for i in range(4)
+    )
+    at = 4 * WIDTH
+    enter = coarse_ref[at : at + 2 * ROWS, : 2 * BLOCKS]
+    leave_high = coarse_ref[at + 2 * ROWS : at + 2 * ROWS + BLOCKS, : 2 * ROWS]
+    leave_low = coarse_ref[at + 2 * ROWS : at + 2 * ROWS + BLOCKS, 2 * ROWS :]
+    leave = jnp.concatenate([leave_high, leave_high, leave_low], axis=1)
     sequences = x_ref.shape[0] // BLOCKS
-    turn_cos, turn_sin = cos_ref[...], sin_ref[...]
+    turn_cos, turn_sin = fine_ref[:ROWS], fine_ref[ROWS:]
     signals = []
     for one in range(sequences):
         rows = slice(one * BLOCKS, (one + 1) * BLOCKS)
@@ -79,7 +93,7 @@
     signals.append(x_ref[:BLOCKS, 2 * WIDTH :])
     count = len(signals)
     signals = jnp.concatenate(signals, axis=1)
-    first = dot(enter_ref[...], jnp.concatenate([signals, signals], axis=0))
+    first = dot(enter, jnp.concatenate([signals, signals], axis=0))
     parts = []
     for i in range(count):
         real = first[:ROWS, i * WIDTH : (i + 1) * WIDTH]
@@ -91,8 +105,8 @@
         )
     spectra = turn_by(
         jnp.concatenate(parts, axis=0),
-        complex_table(table_ref[0], -table_ref[2]),
-        complex_table(table_ref[1], -table_ref[3]),
+        complex_table(cos_high, -sin_high),
+        complex_table(cos_low, -sin_low),
     )
 
     def spectrum(i):
@@ -134,8 +148,8 @@
     parts.append(total)
     back = turn_by(
         jnp.concatenate(parts, axis=0),
-        complex_table(table_ref[0], table_ref[2]),
-        complex_table(table_ref[1], table_ref[3]),
+        complex_table(cos_high, sin_high),
+        complex_table(cos_low, sin_low),
     )
     turned = []
     for i in range(count):
@@ -147,22 +161,63 @@
             )
         )
     high, low = halves(jnp.concatenate(turned, axis=1))
-    values = dot(leave_ref[...], jnp.concatenate([high, low, high], axis=0)).astype(jnp.bfloat16)
+    values = dot(leave, jnp.concatenate([high, low, high], axis=0)).astype(jnp.bfloat16)
     for one in range(sequences):
         rows = slice(one * BLOCKS, (one + 1) * BLOCKS)
         out_ref[rows, : 2 * WIDTH] = values[:, 2 * one * WIDTH : 2 * (one + 1) * WIDTH]
         out_ref[rows, 2 * WIDTH :] = values[:, (count - 1) * WIDTH :]
 
 
-def convolve(rows_in):
+def convolve(rows_in, held):
     return pl.pallas_call(
         convolve_kernel,
         out_shape=jax.ShapeDtypeStruct(rows_in.shape, jnp.bfloat16),
-        in_specs=[pl.BlockSpec(memory_space=pltpu.VMEM)] * 6,
+        in_specs=[pl.BlockSpec(memory_space=pltpu.VMEM)] * 3,
         out_specs=pl.BlockSpec(memory_space=pltpu.VMEM),
         compiler_params=pltpu.CompilerParams(vmem_limit_bytes=32 * 1024 * 1024),
         name="convolve",
-    )(rows_in, *(jnp.asarray(t) for t in tables()))
+    )(rows_in, *held)
+
+
+def flip(array):
+    size = array.shape[1]
+    row = lax.broadcasted_iota(jnp.int32, (size, size), 0)
+    column = lax.broadcasted_iota(jnp.int32, (size, size), 1)
+    identity = jnp.where(row == column, 1.0, 0.0).astype(jnp.bfloat16)
+    return lax.dot_general(
+        identity, array, (((1,), (1,)), ((), ())), preferred_element_type=jnp.float32
+    )
+
+
+def pack_kernel(mixed_ref, gated_ref, filter_ref, coarse_ref, fine_ref, packed_ref, *held_refs):
+    held_coarse_ref, held_fine_ref = held_refs
+    for at, part_ref in enumerate((mixed_ref, gated_ref, filter_ref)):
+        packed_ref[:, at * WIDTH : (at + 1) * WIDTH] = flip(part_ref[...]).astype(jnp.bfloat16)
+    half = WIDTH // 2
+    odd = lax.broadcasted_iota(jnp.int32, (half, WIDTH), 1) % 2 == 1
+    for i in range(4):
+        rows = coarse_ref[i * half : (i + 1) * half].astype(jnp.float32)
+        both = jnp.concatenate([rows, jnp.where(odd, -rows, rows)], axis=0)
+        held_coarse_ref[i * WIDTH : (i + 1) * WIDTH] = both.astype(jnp.bfloat16)
+    held_coarse_ref[4 * WIDTH :] = coarse_ref[4 * half :]
+    held_fine_ref[...] = fine_ref[...]
+
+
+def pack(mixed_in, gated_grad, long_filter):
+    coarse, fine = (jnp.asarray(t) for t in tables())
+    packed, *held = pl.pallas_call(
+        pack_kernel,
+        out_shape=[
+            jax.ShapeDtypeStruct((WIDTH, 3 * WIDTH), jnp.bfloat16),
+            jax.ShapeDtypeStruct((coarse.shape[0] + 2 * WIDTH, WIDTH), jnp.bfloat16),
+            jax.ShapeDtypeStruct(fine.shape, jnp.float32),
+        ],
+        in_specs=[pl.BlockSpec(memory_space=pltpu.VMEM)] * 5,
+        out_specs=[pl.BlockSpec(memory_space=pltpu.VMEM)] * 3,
+        compiler_params=pltpu.CompilerParams(vmem_limit_bytes=32 * 1024 * 1024),
+        name="pack",
+    )(mixed_in, gated_grad, long_filter, coarse, fine)
+    return packed, held
 
 
 def exchange(rows):
@@ -179,9 +234,9 @@
     grad_wide = grad_out[0].astype(jnp.float32)
     mixed_in = (key_wide * values_wide).astype(jnp.bfloat16)
     gated_grad = (grad_wide * query_gate[0].astype(jnp.float32)).astype(jnp.bfloat16)
-    packed = jnp.concatenate([mixed_in.T, gated_grad.T, long_filter.T], axis=1)
+    packed, held = pack(mixed_in, gated_grad, long_filter)
     moved = exchange(packed)
-    result = convolve(moved)
+    result = convolve(moved, held)
     returned = exchange(result)
     part = returned[:, 2 * WIDTH :]
     other = lax.ppermute(part, CORE, [(0, 1), (1, 0)])

time: 77.9 us -> 76.9 us (0.987)
  local copies, waits for them, and re-layouts: 2.13 us -> 0.82 us
    convert_element_type x0 -> x1, other arithmetic: none -> 1.22 us  [body(): (grad_wide * query_gate[0].astype(jnp.float32)).astype(jnp.bfloat16)]
    transpose x1 -> x0, other arithmetic: 1.2 us -> none  [body(): packed = jnp.concatenate([mixed_in.T, gated_grad.T, long_filter.T], axis=1)]
    unnamed x19 -> x13, local copies, waits for them, and re-layouts: 1.05 us -> 0.14 us
where the time goes in v3:
time: 76.9 us; the launch traced here: 76.6 us
  blocking collectives  63.3 us (82%)
  starting transfers between devices  5.83 us (8%)
  Pallas kernels  2.99 us (4%)
  other arithmetic  2.78 us (4%)
  local copies, waits for them, and re-layouts  0.82 us (1%)
  between operations  0.77 us (1%)
    all_to_all x2, blocking collectives, exchange(): lax.all_to_all(rows.reshape(count, 2, width // 2), GROUP, split_axis=0, c...  63.3 us
    ppermute x1, starting transfers between devices, body(): other = lax.ppermute(part, CORE, [(0, 1), (1, 0)])  5.83 us
    pallas_call x1, Pallas kernels, convolve(): pl.pallas_call(convolve_kernel, out_shape=jax.ShapeDtypeStruct(rows_in.sh...  2.68 us
  transfers between devices with their start and end apart: 1, of which 1 were waited for; matrix products, arithmetic and copies ran while one was open for 1% of the time, Pallas kernels for 0%

profile of v3, /device:TPU:1, one launch (start us, length us, event | category | flops | bytes accessed | tf_op | source)
XLA Modules:
  0.0 76.6 jit_solution(3291177140454412418)
XLA Ops:
  0.6 0.0 copy-start
  0.6 0.0 copy-start.2
  0.7 0.0 copy-start.1
  0.7 1.2 %fusion = (bf16[256,256]{1,0:T(8,128)(2,1)S(1)}, bf16[256,256]{1,0:T(8,128)(2,1)S(1)}) fusion(bf16[1,256,256]{2,1,0:T(8,128)(2,1)} %param.7, bf16[1,256,256]{2,1,0:T(8,128)(2,1)} %param.10, bf16[1,256,256]{2,1,0:T(8,128)(2,1)} %param.9, bf16[1,256,256]{2,1,0:T(8,128)(2,1)} %param.8), kind=kLoop, calls=%fused_computation.5 | loop fusion | flops 524288 | bytes 786432 | tf_op jit(solution)/shard_map/convert_element_type | solution.py:236
  1.9 0.0 copy-done
  1.9 0.0 copy-done.2
  1.9 0.1 copy-done.1
  2.0 0.3 pack.1
  2.3 0.1 reshape.28
  2.4 38.2 %all_to_all.10 = bf16[256,2,384]{2,1,0:T(2,128)(2,1)S(1)} all-to-all(bf16[256,2,384]{2,1,0:T(2,128)(2,1)S(1)} %reshape.28), channel_id=1, replica_groups=mesh['hi'=4,'core'=2,'lo'=2,'y'=8,'x'=4] {'hi','lo','y','x'}, dimensions={0} | all-to-all | bytes 786432 | tf_op jit(solution)/shard_map/all_to_all | solution.py:225
  40.6 0.1 copy.12
  40.7 2.7 %convolve.1 = bf16[256,768]{1,0:T(8,128)(2,1)S(1)} custom-call(bf16[256,768]{1,0:T(8,128)(2,1)S(1)} %bitcast.37, bf16[1216,256]{1,0:T(8,128)(2,1)S(1)} %get-tuple-element.8.coarse_ref, f32[128,256]{1,0:T(8,128)S(1)} %get-tuple-element.9.fine_ref), custom_call_target="tpu_custom_call" | custom-call | tf_op jit(solution)/shard_map/convolve/pallas_call | solution.py:172
  43.4 0.1 reshape.30
  43.5 25.1 %all_to_all.11 = bf16[256,2,384]{2,1,0:T(2,128)(2,1)S(1)} all-to-all(bf16[256,2,384]{2,1,0:T(2,128)(2,1)S(1)} %reshape.30), channel_id=1, replica_groups=mesh['hi'=4,'core'=2,'lo'=2,'y'=8,'x'=4] {'hi','lo','y','x'}, dimensions={0} | all-to-all | bytes 786432 | tf_op jit(solution)/shard_map/all_to_all | solution.py:225
  68.6 0.0 copy-start.5
  68.6 0.5 copy.11
  69.1 0.0 copy-start.3
  69.1 0.0 copy-start.4
  69.1 5.8 %collective-permute-start = (bf16[256,256]{0,1:T(8,128)(2,1)S(1)}, bf16[256,256]{0,1:T(8,128)(2,1)S(1)}, u32[]{:S(2)}, u32[]{:S(2)}) collective-permute-start(bf16[256,256]{0,1:T(8,128)(2,1)S(1)} %slice.14), channel_id=1, source_target_pairs={{0,64},{64,0},{1,65},{65,1},{2,66},{66,2},{3,67},{67,3},{4,68},{68... | collective-permute-start | bytes 393224 | tf_op jit(solution)/shard_map/ppermute | solution.py:242
  74.9 0.0 copy-done.5
  74.9 0.0 copy-done.3
  75.0 0.0 copy-done.4
  75.0 0.8 %fusion.5 = (bf16[1,256,256]{2,1,0:T(8,128)(2,1)}, bf16[1,256,256]{2,1,0:T(8,128)(2,1)}, bf16[1,256,256]{2,1,0:T(8,128)(2,1)}) fusion(bf16[1,256,256]{2,1,0:T(8,128)(2,1)S(1)} %copy-done.3, bf16[256,768]{0,1:T(8,128)(2,1)S(1)} %bitcast.39, bf16[1,256,256]{2,1,0:T(8,128)(2,1)S(1)} %copy-done.5, bf16[1,256,256]{2,1,0:T(8,128)(2,1)S(1)} %copy-done.4), kind=kLoop, calls=%fused_computation.11 | loop fusion | flops 720896 | bytes 1048576 | tf_op jit(solution)/shard_map/broadcast_in_dim | solution.py:249
  75.8 0.1 collective-permute-done
  75.9 0.7 add_bitcast_fusion
  (1 shorter events, 0.0 us)
Async XLA Ops:
  0.6 1.3 %copy-start = (bf16[704,256]{1,0:T(8,128)(2,1)S(1)}, bf16[704,256]{1,0:T(8,128)(2,1)}, u32[]{:S(2)}) copy-start(bf16[704,256]{1,0:T(8,128)(2,1)} %constant.4.clone.coarse_ref) | copy-start | bytes 1081348
  0.6 1.3 %copy-start.2 = (f32[128,256]{1,0:T(8,128)S(1)}, f32[128,256]{1,0:T(8,128)}, u32[]{:S(2)}) copy-start(f32[128,256]{1,0:T(8,128)} %constant.5.clone.fine_ref) | copy-start | bytes 393220
  0.7 1.3 %copy-start.1 = (bf16[256,256]{1,0:T(8,128)(2,1)S(1)}, bf16[256,256]{1,0:T(8,128)(2,1)}, u32[]{:S(2)}) copy-start(bf16[256,256]{1,0:T(8,128)(2,1)} %filter_ref.1) | copy-start | bytes 393220
  68.6 6.4 %copy-start.5 = (bf16[1,256,256]{2,1,0:T(8,128)(2,1)S(1)}, bf16[1,256,256]{2,1,0:T(8,128)(2,1)}, u32[]{:S(2)}) copy-start(bf16[1,256,256]{2,1,0:T(8,128)(2,1)} %param.9) | copy-start | bytes 393220
  69.1 5.9 %copy-start.3 = (bf16[1,256,256]{2,1,0:T(8,128)(2,1)S(1)}, bf16[1,256,256]{2,1,0:T(8,128)(2,1)}, u32[]{:S(2)}) copy-start(bf16[1,256,256]{2,1,0:T(8,128)(2,1)} %param.8) | copy-start | bytes 393220
  69.1 5.9 %copy-start.4 = (bf16[1,256,256]{2,1,0:T(8,128)(2,1)S(1)}, bf16[1,256,256]{2,1,0:T(8,128)(2,1)}, u32[]{:S(2)}) copy-start(bf16[1,256,256]{2,1,0:T(8,128)(2,1)} %param.10) | copy-start | bytes 393220
  69.1 6.8 %collective-permute-start = (bf16[256,256]{0,1:T(8,128)(2,1)S(1)}, bf16[256,256]{0,1:T(8,128)(2,1)S(1)}, u32[]{:S(2)}, u32[]{:S(2)}) collective-permute-start(bf16[256,256]{0,1:T(8,128)(2,1)S(1)} %slice.14), channel_id=1, source_target_pairs={{0,64},{64,0},{1,65},{65,1},{2,66},{66,2},{3,67},{67,3},{4,68},{68... | collective-permute-start | bytes 393224 | tf_op jit(solution)/shard_map/ppermute | solution.py:242

commit v4 on v3

--- a/solution.py
+++ b/solution.py
@@ -75,7 +75,7 @@
     )
 
 
-def convolve_kernel(x_ref, coarse_ref, fine_ref, out_ref):
+def convolve_kernel(x_ref, coarse_ref, fine_ref, out_ref, part_ref):
     cos_high, cos_low, sin_high, sin_low = (
         coarse_ref[i * WIDTH : (i + 1) * WIDTH] for i in range(4)
     )
@@ -161,22 +161,61 @@
             )
         )
     high, low = halves(jnp.concatenate(turned, axis=1))
-    values = dot(leave, jnp.concatenate([high, low, high], axis=0)).astype(jnp.bfloat16)
+    values = dot(leave, jnp.concatenate([high, low, high], axis=0))
     for one in range(sequences):
         rows = slice(one * BLOCKS, (one + 1) * BLOCKS)
-        out_ref[rows, : 2 * WIDTH] = values[:, 2 * one * WIDTH : 2 * (one + 1) * WIDTH]
-        out_ref[rows, 2 * WIDTH :] = values[:, (count - 1) * WIDTH :]
+        columns = slice(2 * one * WIDTH, 2 * (one + 1) * WIDTH)
+        out_ref[rows] = values[:, columns].astype(jnp.bfloat16)
+    part_ref[...] = values[:, (count - 1) * WIDTH :]
+
+
+def local_call(kernel, name, outputs, *operands):
+    return pl.pallas_call(
+        kernel,
+        out_shape=[jax.ShapeDtypeStruct(shape, dtype) for shape, dtype in outputs],
+        in_specs=[pl.BlockSpec(memory_space=pltpu.VMEM)] * len(operands),
+        out_specs=[pl.BlockSpec(memory_space=pltpu.VMEM)] * len(outputs),
+        compiler_params=pltpu.CompilerParams(vmem_limit_bytes=32 * 1024 * 1024),
+        name=name,
+    )(*operands)
 
 
 def convolve(rows_in, held):
-    return pl.pallas_call(
-        convolve_kernel,
-        out_shape=jax.ShapeDtypeStruct(rows_in.shape, jnp.bfloat16),
-        in_specs=[pl.BlockSpec(memory_space=pltpu.VMEM)] * 3,
-        out_specs=pl.BlockSpec(memory_space=pltpu.VMEM),
-        compiler_params=pltpu.CompilerParams(vmem_limit_bytes=32 * 1024 * 1024),
-        name="convolve",
-    )(rows_in, *held)
+    outputs = [((rows_in.shape[0], 2 * WIDTH), jnp.bfloat16), ((BLOCKS, WIDTH), jnp.float32)]
+    return local_call(convolve_kernel, "convolve", outputs, rows_in, *held)
+
+
+def merge_kernel(rows_ref, part_ref, other_ref, *refs):
+    count = len(refs) // 2
+    out_ref = refs[count]
+    total = (part_ref[...] + other_ref[...]).astype(jnp.bfloat16)
+    out_ref[:, : 2 * WIDTH] = rows_ref[...]
+    for at in range(0, rows_ref.shape[0], BLOCKS):
+        out_ref[at : at + BLOCKS, 2 * WIDTH :] = total
+    for source, target in zip(refs[:count], refs[count + 1 :]):
+        target[...] = source[...]
+
+
+def merge(rows, part, other, *arrays):
+    outputs = [((rows.shape[0], 3 * WIDTH), jnp.bfloat16)]
+    outputs += [(array.shape, array.dtype) for array in arrays]
+    return local_call(merge_kernel, "merge", outputs, rows, part, other, *arrays)
+
+
+def finish_kernel(
+    rows_ref, key_ref, values_ref, grad_ref, query_out, key_out, value_out, filter_out
+):
+    conv_out = flip(rows_ref[:, :WIDTH])
+    query_out[0] = (grad_ref[0].astype(jnp.float32) * conv_out).astype(jnp.bfloat16)
+    grad_mixed = flip(rows_ref[:, WIDTH : 2 * WIDTH])
+    key_out[0] = (grad_mixed * values_ref[0].astype(jnp.float32)).astype(jnp.bfloat16)
+    value_out[0] = (grad_mixed * key_ref[0].astype(jnp.float32)).astype(jnp.bfloat16)
+    filter_out[...] = flip(rows_ref[:, 2 * WIDTH :])
+
+
+def finish(rows, *arrays):
+    outputs = [(array.shape, jnp.bfloat16) for array in arrays] + [((WIDTH, WIDTH), jnp.float32)]
+    return local_call(finish_kernel, "finish", outputs, rows, *arrays)
 
 
 def flip(array):
@@ -229,24 +268,17 @@
 
 
 def body(query_gate, key_gate, values_in, grad_out, long_filter):
-    key_wide = key_gate[0].astype(jnp.float32)
-    values_wide = values_in[0].astype(jnp.float32)
-    grad_wide = grad_out[0].astype(jnp.float32)
-    mixed_in = (key_wide * values_wide).astype(jnp.bfloat16)
-    gated_grad = (grad_wide * query_gate[0].astype(jnp.float32)).astype(jnp.bfloat16)
+    mixed_in = (key_gate[0].astype(jnp.float32) * values_in[0].astype(jnp.float32)).astype(
+        jnp.bfloat16
+    )
+    gated_grad = (grad_out[0].astype(jnp.float32) * query_gate[0].astype(jnp.float32)).astype(
+        jnp.bfloat16
+    )
     packed, held = pack(mixed_in, gated_grad, long_filter)
-    moved = exchange(packed)
-    result = convolve(moved, held)
-    returned = exchange(result)
-    part = returned[:, 2 * WIDTH :]
+    result, part = convolve(exchange(packed), held)
     other = lax.ppermute(part, CORE, [(0, 1), (1, 0)])
-    conv_out = returned[:, :WIDTH].T.astype(jnp.float32)
-    grad_mixed = returned[:, WIDTH : 2 * WIDTH].T.astype(jnp.float32)
-    grad_query = (grad_wide * conv_out).astype(jnp.bfloat16)
-    grad_key = (grad_mixed * values_wide).astype(jnp.bfloat16)
-    grad_value = (grad_mixed * key_wide).astype(jnp.bfloat16)
-    grad_filter = (part.astype(jnp.float32) + other.astype(jnp.float32)).T
-    return (grad_query[None], grad_key[None], grad_value[None], grad_filter)
+    merged, *arrays = merge(result, part, other, key_gate, values_in, grad_out)
+    return tuple(finish(exchange(merged), *arrays))
 
 
 def solution(mesh):

time: 76.9 us -> 76.3 us (level); the launches traced: 76.6 us -> 75 us
  other arithmetic: 2.78 us -> 1.22 us
  Pallas kernels: 2.99 us -> 4.15 us
  starting transfers between devices: 5.83 us -> 4.99 us
  waiting for transfers between devices: 0.11 us -> 0.88 us
    pallas_call x1 -> x3, Pallas kernels: 2.68 us -> 3.84 us  [local_call(): pl.pallas_call(kernel, out_shape=[jax.ShapeDtypeStruct(shape, dtype) for...]
    ppermute x1, starting transfers between devices: 5.83 us -> 4.99 us  [body(): other = lax.ppermute(part, CORE, [(0, 1), (1, 0)])]
    broadcast_in_dim x1 -> x0, other arithmetic: 0.82 us -> none  [body(): return (grad_query[None], grad_key[None], grad_value[None], grad_filter)]
  transfers between devices with their start and end apart: 1 -> 1, of which waited for: 1 -> 1; matrix products, arithmetic and copies ran while one was open for 1% -> 0% of each run, Pallas kernels for 0% -> 0%
where the time goes in v4:
time: 76.3 us; the launch traced here: 75 us
  blocking collectives  62.7 us (82%)
  starting transfers between devices  4.99 us (7%)
  Pallas kernels  4.15 us (5%)
  other arithmetic  1.22 us (2%)
  waiting for transfers between devices  0.88 us (1%)
    all_to_all x2, blocking collectives, exchange(): lax.all_to_all(rows.reshape(count, 2, width // 2), GROUP, split_axis=0, c...  62.7 us
    ppermute x1, starting transfers between devices, body(): other = lax.ppermute(part, CORE, [(0, 1), (1, 0)])  4.99 us
    pallas_call x3, Pallas kernels, local_call(): pl.pallas_call(kernel, out_shape=[jax.ShapeDtypeStruct(shape, dtype) for...  3.84 us
  transfers between devices with their start and end apart: 1, of which 1 were waited for; matrix products, arithmetic and copies ran while one was open for 0% of the time, Pallas kernels for 0%

profile of v4, /device:TPU:1, one launch (start us, length us, event | category | flops | bytes accessed | tf_op | source)
XLA Modules:
  0.0 75.0 jit_solution(11889957040899477921)
XLA Ops:
  0.6 0.0 copy-start.3
  0.6 0.0 copy-start.5
  0.7 0.0 copy-start.4
  0.7 1.2 %fusion = (bf16[256,256]{1,0:T(8,128)(2,1)S(1)}, bf16[256,256]{1,0:T(8,128)(2,1)S(1)}) fusion(bf16[1,256,256]{2,1,0:T(8,128)(2,1)} %refs_1_.1, bf16[1,256,256]{2,1,0:T(8,128)(2,1)} %refs_0_.1, bf16[1,256,256]{2,1,0:T(8,128)(2,1)} %param.7, bf16[1,256,256]{2,1,0:T(8,128)(2,1)} %refs_2_.1), kind=kLoop, calls=%fused_computation.2 | loop fusion | flops 524288 | bytes 786432 | tf_op jit(solution)/shard_map/convert_element_type | solution.py:271
  1.9 0.0 copy-done.3
  1.9 0.0 copy-done.5
  1.9 0.1 copy-done.4
  2.0 0.3 pack.1
  2.3 0.1 reshape.28
  2.4 38.2 %all_to_all.10 = bf16[256,2,384]{2,1,0:T(2,128)(2,1)S(1)} all-to-all(bf16[256,2,384]{2,1,0:T(2,128)(2,1)S(1)} %reshape.28), channel_id=1, replica_groups=mesh['hi'=4,'core'=2,'lo'=2,'y'=8,'x'=4] {'hi','lo','y','x'}, dimensions={0} | all-to-all | bytes 786432 | tf_op jit(solution)/shard_map/all_to_all | solution.py:264
  40.6 0.1 copy.11
  40.7 0.0 copy-start
  40.7 0.0 copy-start.1
  40.7 0.0 copy-start.2
  40.7 2.7 %convolve.1 = (bf16[256,512]{1,0:T(8,128)(2,1)S(1)}, f32[64,256]{1,0:T(8,128)S(1)}) custom-call(bf16[256,768]{1,0:T(8,128)(2,1)S(1)} %bitcast.9, bf16[1216,256]{1,0:T(8,128)(2,1)S(1)} %get-tuple-element.14.coarse_ref, f32[128,256]{1,0:T(8,128)S(1)} %get-tuple-element.15.fine_ref), custom_call_target="tpu_custom_call" | custom-call | tf_op jit(solution)/shard_map/convolve/pallas_call | solution.py:173
  43.4 5.0 %collective-permute-start = (f32[64,256]{1,0:T(8,128)S(1)}, f32[64,256]{1,0:T(8,128)S(1)}, u32[]{:S(2)}, u32[]{:S(2)}) collective-permute-start(f32[64,256]{1,0:T(8,128)S(1)} %get-tuple-element.17.part_ref), channel_id=1, source_target_pairs={{0,64},{64,0},{1,65},{65,1},{2,66},{66,2},{3,67},{67,3},{4,68},{68... | collective-permute-start | bytes 196616 | tf_op jit(solution)/shard_map/ppermute | solution.py:279
  48.4 0.9 %collective-permute-done.other_ref = f32[64,256]{1,0:T(8,128)S(1)} collective-permute-done((f32[64,256]{1,0:T(8,128)S(1)}, f32[64,256]{1,0:T(8,128)S(1)}, u32[]{:S(2)}, u32[]{:S(2)}) %collective-permute-start) | collective-permute-done | bytes 65568 | tf_op jit(solution)/shard_map/ppermute | solution.py:279
  49.3 0.0 copy-done
  49.3 0.0 copy-done.1
  49.3 0.0 copy-done.2
  49.3 0.1 merge.1
  49.3 0.1 reshape.30
  49.4 24.5 %all_to_all.11 = bf16[256,2,384]{2,1,0:T(2,128)(2,1)S(1)} all-to-all(bf16[256,2,384]{2,1,0:T(2,128)(2,1)S(1)} %reshape.30), channel_id=1, replica_groups=mesh['hi'=4,'core'=2,'lo'=2,'y'=8,'x'=4] {'hi','lo','y','x'}, dimensions={0} | all-to-all | bytes 786432 | tf_op jit(solution)/shard_map/all_to_all | solution.py:264
  73.9 0.1 copy.12
  73.9 1.1 %finish.1 = (bf16[1,256,256]{2,1,0:T(8,128)(2,1)}, bf16[1,256,256]{2,1,0:T(8,128)(2,1)}, bf16[1,256,256]{2,1,0:T(8,128)(2,1)}, f32[256,256]{1,0:T(8,128)}) custom-call(bf16[256,768]{1,0:T(8,128)(2,1)S(1)} %bitcast.8, bf16[1,256,256]{2,1,0:T(8,128)(2,1)S(1)} %get-tuple-element.19.key_ref, bf16[1,256,256]{2,1,0:T(8,128)(2,1)S(1)} %get-tuple-element.20.values_ref, ...), custom_call_target="tpu_custom_call" | custom-call | tf_op jit(solution)/shard_map/finish/pallas_call | solution.py:173
Async XLA Ops:
  0.6 1.3 %copy-start.3 = (bf16[704,256]{1,0:T(8,128)(2,1)S(1)}, bf16[704,256]{1,0:T(8,128)(2,1)}, u32[]{:S(2)}) copy-start(bf16[704,256]{1,0:T(8,128)(2,1)} %constant.4.clone.coarse_ref) | copy-start | bytes 1081348
  0.6 1.3 %copy-start.5 = (f32[128,256]{1,0:T(8,128)S(1)}, f32[128,256]{1,0:T(8,128)}, u32[]{:S(2)}) copy-start(f32[128,256]{1,0:T(8,128)} %constant.5.clone.fine_ref) | copy-start | bytes 393220
  0.7 1.3 %copy-start.4 = (bf16[256,256]{1,0:T(8,128)(2,1)S(1)}, bf16[256,256]{1,0:T(8,128)(2,1)}, u32[]{:S(2)}) copy-start(bf16[256,256]{1,0:T(8,128)(2,1)} %filter_ref.1) | copy-start | bytes 393220
  40.7 8.6 %copy-start = (bf16[1,256,256]{2,1,0:T(8,128)(2,1)S(1)}, bf16[1,256,256]{2,1,0:T(8,128)(2,1)}, u32[]{:S(2)}) copy-start(bf16[1,256,256]{2,1,0:T(8,128)(2,1)} %refs_1_.1) | copy-start | bytes 393220
  40.7 8.6 %copy-start.1 = (bf16[1,256,256]{2,1,0:T(8,128)(2,1)S(1)}, bf16[1,256,256]{2,1,0:T(8,128)(2,1)}, u32[]{:S(2)}) copy-start(bf16[1,256,256]{2,1,0:T(8,128)(2,1)} %refs_0_.1) | copy-start | bytes 393220
  40.7 8.6 %copy-start.2 = (bf16[1,256,256]{2,1,0:T(8,128)(2,1)S(1)}, bf16[1,256,256]{2,1,0:T(8,128)(2,1)}, u32[]{:S(2)}) copy-start(bf16[1,256,256]{2,1,0:T(8,128)(2,1)} %refs_2_.1) | copy-start | bytes 393220
  43.4 5.9 %collective-permute-start = (f32[64,256]{1,0:T(8,128)S(1)}, f32[64,256]{1,0:T(8,128)S(1)}, u32[]{:S(2)}, u32[]{:S(2)}) collective-permute-start(f32[64,256]{1,0:T(8,128)S(1)} %get-tuple-element.17.part_ref), channel_id=1, source_target_pairs={{0,64},{64,0},{1,65},{65,1},{2,66},{66,2},{3,67},{67,3},{4,68},{68... | collective-permute-start | bytes 196616 | tf_op jit(solution)/shard_map/ppermute | solution.py:279

commit v5 on v4

--- a/solution.py
+++ b/solution.py
@@ -11,7 +11,7 @@
 HI, CORE, LO, Y, X = "hi", "core", "lo", "y", "x"
 SIZES = (4, 2, 2, 8, 4)
 SEQ_AXES = (LO, Y, X)
-GROUP = (HI, LO, Y, X)
+AXES = (HI, CORE, LO, Y, X)
 BLOCKS = 64
 WIDTH = 256
 ROWS = 64
@@ -36,15 +36,16 @@
     angle = 2.0 * math.pi * (place[:, None] * place[None, :] % WIDTH) / WIDTH
     cos_high, cos_low = split_bf16(np.cos(angle).astype(np.float32))
     sin_high, sin_low = split_bf16(np.sin(angle).astype(np.float32))
-    enter = np.concatenate(split_bf16(enter), axis=1)
+    forward, backward = enter, enter[:, ::-1]
     coarse = np.concatenate(
         [
             cos_high[: WIDTH // 2],
             cos_low[: WIDTH // 2],
             sin_high[: WIDTH // 2],
             sin_low[: WIDTH // 2],
-            np.pad(enter, ((0, 0), (0, WIDTH - enter.shape[1]))),
+            np.concatenate(split_bf16(forward) + split_bf16(backward), axis=1),
             np.concatenate(split_bf16(leave), axis=1),
+            np.concatenate(split_bf16(leave[::-1]), axis=1),
         ],
         axis=0,
     )
@@ -80,10 +81,19 @@
         coarse_ref[i * WIDTH : (i + 1) * WIDTH] for i in range(4)
     )
     at = 4 * WIDTH
-    enter = coarse_ref[at : at + 2 * ROWS, : 2 * BLOCKS]
-    leave_high = coarse_ref[at + 2 * ROWS : at + 2 * ROWS + BLOCKS, : 2 * ROWS]
-    leave_low = coarse_ref[at + 2 * ROWS : at + 2 * ROWS + BLOCKS, 2 * ROWS :]
-    leave = jnp.concatenate([leave_high, leave_high, leave_low], axis=1)
+    backward = runs_backward()
+    enter = jnp.where(
+        backward,
+        coarse_ref[at : at + 2 * ROWS, 2 * BLOCKS :],
+        coarse_ref[at : at + 2 * ROWS, : 2 * BLOCKS],
+    )
+    at += 2 * ROWS
+    natural = coarse_ref[at : at + BLOCKS]
+    leave = jnp.where(backward, coarse_ref[at + BLOCKS : at + 2 * BLOCKS], natural)
+    natural, leave = (
+        jnp.concatenate([both[:, : 2 * ROWS], both[:, : 2 * ROWS], both[:, 2 * ROWS :]], axis=1)
+        for both in (natural, leave)
+    )
     sequences = x_ref.shape[0] // BLOCKS
     turn_cos, turn_sin = fine_ref[:ROWS], fine_ref[ROWS:]
     signals = []
@@ -161,12 +171,14 @@
             )
         )
     high, low = halves(jnp.concatenate(turned, axis=1))
-    values = dot(leave, jnp.concatenate([high, low, high], axis=0))
+    turned = jnp.concatenate([high, low, high], axis=0)
+    last = (count - 1) * WIDTH
+    values = dot(leave, turned[:, :last])
     for one in range(sequences):
         rows = slice(one * BLOCKS, (one + 1) * BLOCKS)
         columns = slice(2 * one * WIDTH, 2 * (one + 1) * WIDTH)
         out_ref[rows] = values[:, columns].astype(jnp.bfloat16)
-    part_ref[...] = values[:, (count - 1) * WIDTH :]
+    part_ref[...] = dot(natural, turned[:, last:])
 
 
 def local_call(kernel, name, outputs, *operands):
@@ -189,6 +201,7 @@
     count = len(refs) // 2
     out_ref = refs[count]
     total = (part_ref[...] + other_ref[...]).astype(jnp.bfloat16)
+    total = dot(order(BLOCKS, runs_backward()), total).astype(jnp.bfloat16)
     out_ref[:, : 2 * WIDTH] = rows_ref[...]
     for at in range(0, rows_ref.shape[0], BLOCKS):
         out_ref[at : at + BLOCKS, 2 * WIDTH :] = total
@@ -205,12 +218,14 @@
 def finish_kernel(
     rows_ref, key_ref, values_ref, grad_ref, query_out, key_out, value_out, filter_out
 ):
-    conv_out = flip(rows_ref[:, :WIDTH])
+    rows = dot(order(WIDTH, runs_backward()), rows_ref[...]).astype(jnp.bfloat16)
+    identity = order(WIDTH, False)
+    conv_out = flip(identity, rows[:, :WIDTH])
     query_out[0] = (grad_ref[0].astype(jnp.float32) * conv_out).astype(jnp.bfloat16)
-    grad_mixed = flip(rows_ref[:, WIDTH : 2 * WIDTH])
+    grad_mixed = flip(identity, rows[:, WIDTH : 2 * WIDTH])
     key_out[0] = (grad_mixed * values_ref[0].astype(jnp.float32)).astype(jnp.bfloat16)
     value_out[0] = (grad_mixed * key_ref[0].astype(jnp.float32)).astype(jnp.bfloat16)
-    filter_out[...] = flip(rows_ref[:, 2 * WIDTH :])
+    filter_out[...] = flip(identity, rows[:, 2 * WIDTH :])
 
 
 def finish(rows, *arrays):
@@ -218,20 +233,29 @@
     return local_call(finish_kernel, "finish", outputs, rows, *arrays)
 
 
-def flip(array):
-    size = array.shape[1]
+def order(size, backward):
     row = lax.broadcasted_iota(jnp.int32, (size, size), 0)
     column = lax.broadcasted_iota(jnp.int32, (size, size), 1)
-    identity = jnp.where(row == column, 1.0, 0.0).astype(jnp.bfloat16)
+    match = jnp.where(backward, size - 1 - row, row) == column
+    return jnp.where(match, 1.0, 0.0).astype(jnp.bfloat16)
+
+
+def flip(matrix, array):
     return lax.dot_general(
-        identity, array, (((1,), (1,)), ((), ())), preferred_element_type=jnp.float32
-    )
+        matrix, array, (((1,), (1,)), ((), ())), preferred_element_type=jnp.float32
+    )
+
+
+def runs_backward():
+    return lax.axis_index(CORE) == 1
 
 
 def pack_kernel(mixed_ref, gated_ref, filter_ref, coarse_ref, fine_ref, packed_ref, *held_refs):
     held_coarse_ref, held_fine_ref = held_refs
+    members = order(WIDTH, runs_backward())
     for at, part_ref in enumerate((mixed_ref, gated_ref, filter_ref)):
-        packed_ref[:, at * WIDTH : (at + 1) * WIDTH] = flip(part_ref[...]).astype(jnp.bfloat16)
+        turned = flip(members, part_ref[...])
+        packed_ref[:, at * WIDTH : (at + 1) * WIDTH] = turned.astype(jnp.bfloat16)
     half = WIDTH // 2
     odd = lax.broadcasted_iota(jnp.int32, (half, WIDTH), 1) % 2 == 1
     for i in range(4):
@@ -259,10 +283,20 @@
     return packed, held
 
 
+def member_lists():
+    places = np.arange(math.prod(SIZES)).reshape(SIZES)
+    return [places[:, 0].reshape(-1).tolist(), places[:, 1].reshape(-1)[::-1].tolist()]
+
+
 def exchange(rows):
     count, width = rows.shape
     moved = lax.all_to_all(
-        rows.reshape(count, 2, width // 2), GROUP, split_axis=0, concat_axis=0, tiled=True
+        rows.reshape(count, 2, width // 2),
+        AXES,
+        split_axis=0,
+        concat_axis=0,
+        tiled=True,
+        axis_index_groups=member_lists(),
     )
     return moved.reshape(count, width)
 

time: 76.3 us -> 73.9 us (0.969); the launches traced: 75 us -> 73.5 us
  blocking collectives: 62.7 us -> 60.8 us
    all_to_all x2, blocking collectives: 62.7 us -> 60.8 us  [exchange(): lax.all_to_all(rows.reshape(count, 2, width // 2), AXES, split_axis=0, co...]
where the time goes in v5:
time: 73.9 us; the launch traced here: 73.5 us
  blocking collectives  60.8 us (82%)
  starting transfers between devices  5.12 us (7%)
  Pallas kernels  4.4 us (6%)
  other arithmetic  1.22 us (2%)
  waiting for transfers between devices  0.88 us (1%)
  between operations  0.74 us (1%)
    all_to_all x2, blocking collectives, exchange(): lax.all_to_all(rows.reshape(count, 2, width // 2), AXES, split_axis=0, co...  60.8 us
    ppermute x1, starting transfers between devices, body(): other = lax.ppermute(part, CORE, [(0, 1), (1, 0)])  5.12 us
    pallas_call x3, Pallas kernels, local_call(): pl.pallas_call(kernel, out_shape=[jax.ShapeDtypeStruct(shape, dtype) for...  4.07 us
  transfers between devices with their start and end apart: 1, of which 1 were waited for; matrix products, arithmetic and copies ran while one was open for 0% of the time, Pallas kernels for 0%

profile of v5, /device:TPU:1, one launch (start us, length us, event | category | flops | bytes accessed | tf_op | source)
XLA Modules:
  0.0 73.5 jit_solution(4563525359946513710)
XLA Ops:
  0.6 0.0 copy-start.3
  0.6 0.0 copy-start.5
  0.7 0.0 copy-start.4
  0.7 1.2 %fusion = (bf16[256,256]{1,0:T(8,128)(2,1)S(1)}, bf16[256,256]{1,0:T(8,128)(2,1)S(1)}) fusion(bf16[1,256,256]{2,1,0:T(8,128)(2,1)} %refs_1_.1, bf16[1,256,256]{2,1,0:T(8,128)(2,1)} %refs_0_.1, bf16[1,256,256]{2,1,0:T(8,128)(2,1)} %param.7, bf16[1,256,256]{2,1,0:T(8,128)(2,1)} %refs_2_.1), kind=kLoop, calls=%fused_computation.2 | loop fusion | flops 524288 | bytes 786432 | tf_op jit(solution)/shard_map/convert_element_type | solution.py:305
  1.9 0.0 copy-done.3
  1.9 0.0 copy-done.5
  1.9 0.1 copy-done.4
  2.0 0.3 pack.1
  2.3 0.1 reshape.28
  2.4 35.4 %all_to_all.10 = bf16[256,2,384]{2,1,0:T(2,128)(2,1)S(1)} all-to-all(bf16[256,2,384]{2,1,0:T(2,128)(2,1)S(1)} %reshape.28), channel_id=1, replica_groups={{0,1,2,3,4,5,6,7,8,9,10,11,12,13,14,15,16,17,18,19,20,21,22,23,24,25,26..., dimensions={0} | all-to-all | bytes 786432 | tf_op jit(solution)/shard_map/all_to_all | solution.py:293
  37.8 0.1 copy.11
  37.8 0.0 copy-start
  37.8 0.0 copy-start.1
  37.8 0.0 copy-start.2
  37.8 2.7 %convolve.1 = (bf16[256,512]{1,0:T(8,128)(2,1)S(1)}, f32[64,256]{1,0:T(8,128)S(1)}) custom-call(bf16[256,768]{1,0:T(8,128)(2,1)S(1)} %bitcast.9, bf16[1280,256]{1,0:T(8,128)(2,1)S(1)} %get-tuple-element.14.coarse_ref, f32[128,256]{1,0:T(8,128)S(1)} %get-tuple-element.15.fine_ref), custom_call_target="tpu_custom_call" | custom-call | tf_op jit(solution)/shard_map/convolve/pallas_call | solution.py:185
  40.5 5.1 %collective-permute-start = (f32[64,256]{1,0:T(8,128)S(1)}, f32[64,256]{1,0:T(8,128)S(1)}, u32[]{:S(2)}, u32[]{:S(2)}) collective-permute-start(f32[64,256]{1,0:T(8,128)S(1)} %get-tuple-element.17.part_ref), channel_id=1, source_target_pairs={{0,64},{64,0},{1,65},{65,1},{2,66},{66,2},{3,67},{67,3},{4,68},{68... | collective-permute-start | bytes 196616 | tf_op jit(solution)/shard_map/ppermute | solution.py:313
  45.7 0.9 %collective-permute-done.other_ref = f32[64,256]{1,0:T(8,128)S(1)} collective-permute-done((f32[64,256]{1,0:T(8,128)S(1)}, f32[64,256]{1,0:T(8,128)S(1)}, u32[]{:S(2)}, u32[]{:S(2)}) %collective-permute-start) | collective-permute-done | bytes 65568 | tf_op jit(solution)/shard_map/ppermute | solution.py:313
  46.5 0.0 copy-done
  46.5 0.0 copy-done.1
  46.5 0.0 copy-done.2
  46.5 0.1 merge.1
  46.7 0.1 reshape.30
  46.8 25.4 %all_to_all.11 = bf16[256,2,384]{2,1,0:T(2,128)(2,1)S(1)} all-to-all(bf16[256,2,384]{2,1,0:T(2,128)(2,1)S(1)} %reshape.30), channel_id=1, replica_groups={{0,1,2,3,4,5,6,7,8,9,10,11,12,13,14,15,16,17,18,19,20,21,22,23,24,25,26..., dimensions={0} | all-to-all | bytes 786432 | tf_op jit(solution)/shard_map/all_to_all | solution.py:293
  72.2 0.1 copy.12
  72.3 1.3 %finish.1 = (bf16[1,256,256]{2,1,0:T(8,128)(2,1)}, bf16[1,256,256]{2,1,0:T(8,128)(2,1)}, bf16[1,256,256]{2,1,0:T(8,128)(2,1)}, f32[256,256]{1,0:T(8,128)}) custom-call(bf16[256,768]{1,0:T(8,128)(2,1)S(1)} %bitcast.8, bf16[1,256,256]{2,1,0:T(8,128)(2,1)S(1)} %get-tuple-element.19.key_ref, bf16[1,256,256]{2,1,0:T(8,128)(2,1)S(1)} %get-tuple-element.20.values_ref, ...), custom_call_target="tpu_custom_call" | custom-call | tf_op jit(solution)/shard_map/finish/pallas_call | solution.py:185
Async XLA Ops:
  0.6 1.3 %copy-start.3 = (bf16[768,256]{1,0:T(8,128)(2,1)S(1)}, bf16[768,256]{1,0:T(8,128)(2,1)}, u32[]{:S(2)}) copy-start(bf16[768,256]{1,0:T(8,128)(2,1)} %constant.4.clone.coarse_ref) | copy-start | bytes 1179652
  0.6 1.3 %copy-start.5 = (f32[128,256]{1,0:T(8,128)S(1)}, f32[128,256]{1,0:T(8,128)}, u32[]{:S(2)}) copy-start(f32[128,256]{1,0:T(8,128)} %constant.5.clone.fine_ref) | copy-start | bytes 393220
  0.7 1.3 %copy-start.4 = (bf16[256,256]{1,0:T(8,128)(2,1)S(1)}, bf16[256,256]{1,0:T(8,128)(2,1)}, u32[]{:S(2)}) copy-start(bf16[256,256]{1,0:T(8,128)(2,1)} %filter_ref.1) | copy-start | bytes 393220
  37.8 8.7 %copy-start = (bf16[1,256,256]{2,1,0:T(8,128)(2,1)S(1)}, bf16[1,256,256]{2,1,0:T(8,128)(2,1)}, u32[]{:S(2)}) copy-start(bf16[1,256,256]{2,1,0:T(8,128)(2,1)} %refs_1_.1) | copy-start | bytes 393220
  37.8 8.7 %copy-start.1 = (bf16[1,256,256]{2,1,0:T(8,128)(2,1)S(1)}, bf16[1,256,256]{2,1,0:T(8,128)(2,1)}, u32[]{:S(2)}) copy-start(bf16[1,256,256]{2,1,0:T(8,128)(2,1)} %refs_0_.1) | copy-start | bytes 393220
  37.8 8.7 %copy-start.2 = (bf16[1,256,256]{2,1,0:T(8,128)(2,1)S(1)}, bf16[1,256,256]{2,1,0:T(8,128)(2,1)}, u32[]{:S(2)}) copy-start(bf16[1,256,256]{2,1,0:T(8,128)(2,1)} %refs_2_.1) | copy-start | bytes 393220
  40.5 6.0 %collective-permute-start = (f32[64,256]{1,0:T(8,128)S(1)}, f32[64,256]{1,0:T(8,128)S(1)}, u32[]{:S(2)}, u32[]{:S(2)}) collective-permute-start(f32[64,256]{1,0:T(8,128)S(1)} %get-tuple-element.17.part_ref), channel_id=1, source_target_pairs={{0,64},{64,0},{1,65},{65,1},{2,66},{66,2},{3,67},{67,3},{4,68},{68... | collective-permute-start | bytes 196616 | tf_op jit(solution)/shard_map/ppermute | solution.py:313

commit v6 on v5

--- a/solution.py
+++ b/solution.py
@@ -218,14 +218,13 @@
 def finish_kernel(
     rows_ref, key_ref, values_ref, grad_ref, query_out, key_out, value_out, filter_out
 ):
-    rows = dot(order(WIDTH, runs_backward()), rows_ref[...]).astype(jnp.bfloat16)
-    identity = order(WIDTH, False)
-    conv_out = flip(identity, rows[:, :WIDTH])
+    members = order(WIDTH, runs_backward())
+    conv_out = unflip(rows_ref[:, :WIDTH], members)
     query_out[0] = (grad_ref[0].astype(jnp.float32) * conv_out).astype(jnp.bfloat16)
-    grad_mixed = flip(identity, rows[:, WIDTH : 2 * WIDTH])
+    grad_mixed = unflip(rows_ref[:, WIDTH : 2 * WIDTH], members)
     key_out[0] = (grad_mixed * values_ref[0].astype(jnp.float32)).astype(jnp.bfloat16)
     value_out[0] = (grad_mixed * key_ref[0].astype(jnp.float32)).astype(jnp.bfloat16)
-    filter_out[...] = flip(identity, rows[:, 2 * WIDTH :])
+    filter_out[...] = unflip(rows_ref[:, 2 * WIDTH :], members)
 
 
 def finish(rows, *arrays):
@@ -243,6 +242,12 @@
 def flip(matrix, array):
     return lax.dot_general(
         matrix, array, (((1,), (1,)), ((), ())), preferred_element_type=jnp.float32
+    )
+
+
+def unflip(array, matrix):
+    return lax.dot_general(
+        array, matrix, (((0,), (0,)), ((), ())), preferred_element_type=jnp.float32
     )
 
 

time: 73.9 us -> 73.7 us (level)
  no operation moved by 1% of the time
where the time goes in v6:
time: 73.7 us; the launch traced here: 73.3 us
  blocking collectives  60.8 us (82%)
  starting transfers between devices  5.12 us (7%)
  Pallas kernels  4.22 us (6%)
  other arithmetic  1.22 us (2%)
  waiting for transfers between devices  0.88 us (1%)
  between operations  0.74 us (1%)
    all_to_all x2, blocking collectives, exchange(): lax.all_to_all(rows.reshape(count, 2, width // 2), AXES, split_axis=0, co...  60.8 us
    ppermute x1, starting transfers between devices, body(): other = lax.ppermute(part, CORE, [(0, 1), (1, 0)])  5.12 us
    pallas_call x3, Pallas kernels, local_call(): pl.pallas_call(kernel, out_shape=[jax.ShapeDtypeStruct(shape, dtype) for...  3.89 us
  transfers between devices with their start and end apart: 1, of which 1 were waited for; matrix products, arithmetic and copies ran while one was open for 0% of the time, Pallas kernels for 0%

profile of v6, /device:TPU:1, one launch (start us, length us, event | category | flops | bytes accessed | tf_op | source)
XLA Modules:
  0.0 73.3 jit_solution(10464328836749203308)
XLA Ops:
  0.6 0.0 copy-start.3
  0.6 0.0 copy-start.5
  0.7 0.0 copy-start.4
  0.7 1.2 %fusion = (bf16[256,256]{1,0:T(8,128)(2,1)S(1)}, bf16[256,256]{1,0:T(8,128)(2,1)S(1)}) fusion(bf16[1,256,256]{2,1,0:T(8,128)(2,1)} %refs_1_.1, bf16[1,256,256]{2,1,0:T(8,128)(2,1)} %refs_0_.1, bf16[1,256,256]{2,1,0:T(8,128)(2,1)} %param.7, bf16[1,256,256]{2,1,0:T(8,128)(2,1)} %refs_2_.1), kind=kLoop, calls=%fused_computation.2 | loop fusion | flops 524288 | bytes 786432 | tf_op jit(solution)/shard_map/convert_element_type | solution.py:310
  1.9 0.0 copy-done.3
  1.9 0.0 copy-done.5
  1.9 0.1 copy-done.4
  2.0 0.3 pack.1
  2.3 0.1 reshape.28
  2.4 35.4 %all_to_all.10 = bf16[256,2,384]{2,1,0:T(2,128)(2,1)S(1)} all-to-all(bf16[256,2,384]{2,1,0:T(2,128)(2,1)S(1)} %reshape.28), channel_id=1, replica_groups={{0,1,2,3,4,5,6,7,8,9,10,11,12,13,14,15,16,17,18,19,20,21,22,23,24,25,26..., dimensions={0} | all-to-all | bytes 786432 | tf_op jit(solution)/shard_map/all_to_all | solution.py:298
  37.8 0.1 copy.11
  37.8 0.0 copy-start
  37.8 0.0 copy-start.1
  37.8 0.0 copy-start.2
  37.8 2.7 %convolve.1 = (bf16[256,512]{1,0:T(8,128)(2,1)S(1)}, f32[64,256]{1,0:T(8,128)S(1)}) custom-call(bf16[256,768]{1,0:T(8,128)(2,1)S(1)} %bitcast.9, bf16[1280,256]{1,0:T(8,128)(2,1)S(1)} %get-tuple-element.14.coarse_ref, f32[128,256]{1,0:T(8,128)S(1)} %get-tuple-element.15.fine_ref), custom_call_target="tpu_custom_call" | custom-call | tf_op jit(solution)/shard_map/convolve/pallas_call | solution.py:185
  40.5 5.1 %collective-permute-start = (f32[64,256]{1,0:T(8,128)S(1)}, f32[64,256]{1,0:T(8,128)S(1)}, u32[]{:S(2)}, u32[]{:S(2)}) collective-permute-start(f32[64,256]{1,0:T(8,128)S(1)} %get-tuple-element.17.part_ref), channel_id=1, source_target_pairs={{0,64},{64,0},{1,65},{65,1},{2,66},{66,2},{3,67},{67,3},{4,68},{68... | collective-permute-start | bytes 196616 | tf_op jit(solution)/shard_map/ppermute | solution.py:318
  45.7 0.9 %collective-permute-done.other_ref = f32[64,256]{1,0:T(8,128)S(1)} collective-permute-done((f32[64,256]{1,0:T(8,128)S(1)}, f32[64,256]{1,0:T(8,128)S(1)}, u32[]{:S(2)}, u32[]{:S(2)}) %collective-permute-start) | collective-permute-done | bytes 65568 | tf_op jit(solution)/shard_map/ppermute | solution.py:318
  46.5 0.0 copy-done
  46.5 0.0 copy-done.1
  46.5 0.0 copy-done.2
  46.5 0.1 merge.1
  46.7 0.1 reshape.30
  46.8 25.4 %all_to_all.11 = bf16[256,2,384]{2,1,0:T(2,128)(2,1)S(1)} all-to-all(bf16[256,2,384]{2,1,0:T(2,128)(2,1)S(1)} %reshape.30), channel_id=1, replica_groups={{0,1,2,3,4,5,6,7,8,9,10,11,12,13,14,15,16,17,18,19,20,21,22,23,24,25,26..., dimensions={0} | all-to-all | bytes 786432 | tf_op jit(solution)/shard_map/all_to_all | solution.py:298
  72.2 0.1 copy.12
  72.3 1.1 %finish.1 = (bf16[1,256,256]{2,1,0:T(8,128)(2,1)}, bf16[1,256,256]{2,1,0:T(8,128)(2,1)}, bf16[1,256,256]{2,1,0:T(8,128)(2,1)}, f32[256,256]{1,0:T(8,128)}) custom-call(bf16[256,768]{1,0:T(8,128)(2,1)S(1)} %bitcast.8, bf16[1,256,256]{2,1,0:T(8,128)(2,1)S(1)} %get-tuple-element.19.key_ref, bf16[1,256,256]{2,1,0:T(8,128)(2,1)S(1)} %get-tuple-element.20.values_ref, ...), custom_call_target="tpu_custom_call" | custom-call | tf_op jit(solution)/shard_map/finish/pallas_call | solution.py:185
Async XLA Ops:
  0.6 1.3 %copy-start.3 = (bf16[768,256]{1,0:T(8,128)(2,1)S(1)}, bf16[768,256]{1,0:T(8,128)(2,1)}, u32[]{:S(2)}) copy-start(bf16[768,256]{1,0:T(8,128)(2,1)} %constant.4.clone.coarse_ref) | copy-start | bytes 1179652
  0.6 1.3 %copy-start.5 = (f32[128,256]{1,0:T(8,128)S(1)}, f32[128,256]{1,0:T(8,128)}, u32[]{:S(2)}) copy-start(f32[128,256]{1,0:T(8,128)} %constant.5.clone.fine_ref) | copy-start | bytes 393220
  0.7 1.3 %copy-start.4 = (bf16[256,256]{1,0:T(8,128)(2,1)S(1)}, bf16[256,256]{1,0:T(8,128)(2,1)}, u32[]{:S(2)}) copy-start(bf16[256,256]{1,0:T(8,128)(2,1)} %filter_ref.1) | copy-start | bytes 393220
  37.8 8.7 %copy-start = (bf16[1,256,256]{2,1,0:T(8,128)(2,1)S(1)}, bf16[1,256,256]{2,1,0:T(8,128)(2,1)}, u32[]{:S(2)}) copy-start(bf16[1,256,256]{2,1,0:T(8,128)(2,1)} %refs_1_.1) | copy-start | bytes 393220
  37.8 8.7 %copy-start.1 = (bf16[1,256,256]{2,1,0:T(8,128)(2,1)S(1)}, bf16[1,256,256]{2,1,0:T(8,128)(2,1)}, u32[]{:S(2)}) copy-start(bf16[1,256,256]{2,1,0:T(8,128)(2,1)} %refs_0_.1) | copy-start | bytes 393220
  37.8 8.7 %copy-start.2 = (bf16[1,256,256]{2,1,0:T(8,128)(2,1)S(1)}, bf16[1,256,256]{2,1,0:T(8,128)(2,1)}, u32[]{:S(2)}) copy-start(bf16[1,256,256]{2,1,0:T(8,128)(2,1)} %refs_2_.1) | copy-start | bytes 393220
  40.5 6.0 %collective-permute-start = (f32[64,256]{1,0:T(8,128)S(1)}, f32[64,256]{1,0:T(8,128)S(1)}, u32[]{:S(2)}, u32[]{:S(2)}) collective-permute-start(f32[64,256]{1,0:T(8,128)S(1)} %get-tuple-element.17.part_ref), channel_id=1, source_target_pairs={{0,64},{64,0},{1,65},{65,1},{2,66},{66,2},{3,67},{67,3},{4,68},{68... | collective-permute-start | bytes 196616 | tf_op jit(solution)/shard_map/ppermute | solution.py:318
